TPU v7x, 256 devices: a whole 4x4x8 slice. The times are simulated.
256 devices in a mesh: ia: 8 (over z_hi, x), ja: 32 (over y, z_lo, core).
Axes of the slice: x: 4, y: 4, z: 8 (z_hi: 2, z_lo: 4; z = z_hi * 4 + z_lo), core: 2. Of those that a mesh axis runs over, the one named last changes fastest.
Arguments:
- amplitudes: float32 [64, 64, 8192], P('ia', 'ja'), may hold values from -6 to 6
- residual_in: float32 [64, 64, 8192], P('ia', 'ja'), may hold values from -6 to 6
- ladder_ints: float32 [8192, 8192], P('ja'), may hold values from -0.0625 to 0.0625
- occ_energy: float32 [64], replicated, may hold values from -3 to -0.5
- virt_energy: float32 [256], replicated, may hold values from 0.3 to 3
- virt_order: int32 [256], replicated, may hold values from 0 to 255, each once
Outputs:
- residual: float32 [64, 64, 8192], P('ia', 'ja')
- new_amplitudes: float32 [64, 64, 8192], P('ia', 'ja')
Inputs may be any that keep to these rules, and one draw needn't show every extreme that they name: `virt_order`: each orbital number appears once; entries h * 32 to (h + 1) * 32 - 1 are the virtuals of irrep h.
All inputs are finite; a program needn't handle non-finite values.
Results may differ from a plain program's by a relative error of at most 0.000059.
Values sent between devices are 32-bit elements; how exact they have to be, the bound alone decides.
No kernel may reach another device: no remote copies, remote signals or barrier semaphores. Data moves between devices by JAX's collectives and lax.ppermute only.
A program may use at most 128 MiB of HBM per device.

v0:
```python
import jax
import jax.numpy as jnp
from jax import lax
from jax.experimental import pallas as pl
from jax.experimental.pallas import tpu as pltpu
from jax.sharding import PartitionSpec as P

NV = 256
IRREPS = 8
VH = 32
NP = 8192
HALF = NP // 2
STREAMS = 2
RANGE = NP // (2 * STREAMS)
TILE = 512
ROWS = 256
COLS = 256
BOTH = ("ia", "ja")
F32 = jnp.float32
BF16 = jnp.bfloat16
MULTIPLY_LIMIT = 12
LOADS = 4


def device_at(x, y, z, c):
    z = z % 8
    return (z // 4 * 4 + x % 4) * 32 + (y % 4) * 8 + (z % 4) * 2 + c % 2


def moved(dx=0, dy=0, dz=0, dc=0, way=0):
    pairs = []
    for x in range(4):
        for y in range(4):
            for z in range(8):
                for c in range(2):
                    sign = 1 - 2 * c * way
                    to = device_at(x + sign * dx, y + sign * dy, z + sign * dz, c + dc)
                    pairs.append((device_at(x, y, z, c), to))
    return pairs


def shift(array, **steps):
    return lax.ppermute(array, BOTH, moved(**steps))


def split(value):
    high = value.astype(BF16)
    return high, (value - high.astype(F32)).astype(BF16)


def multiply(pieces, own, partner, start, total):
    dims = (((1,), (1,)), ((), ()))

    def tile(k, carry):
        def columns(first):
            return pl.ds(pl.multiple_of(k * TILE + first, TILE), TILE)

        parts = [ref[row : row + rows, columns(first)] for ref, row, rows, first in pieces]
        t_high, t_low = split(jnp.concatenate(parts, axis=0))
        at = columns(start)
        v_high, v_low = split(jnp.concatenate([own[:, at], partner[:, at]], axis=0))
        part = lax.dot_general(t_high, v_low, dims, preferred_element_type=F32)
        part += lax.dot_general(t_low, v_high, dims, preferred_element_type=F32)
        part += lax.dot_general(t_high, v_high, dims, preferred_element_type=F32)
        total[...] += part
        return carry

    lax.fori_loop(0, RANGE // TILE, tile, 0)


def prepare_kernel(order, energy, pair, turn):
    row = lax.broadcasted_iota(jnp.int32, (NV, NV), 0)
    chosen = (row == order[...]).astype(BF16)
    values, dims = energy[...], (((1,), (0,)), ((), ()))
    grouped = exact(values, chosen, dims)
    lane = lax.broadcasted_iota(jnp.int32, (IRREPS, NV), 1)
    irrep = lax.broadcasted_iota(jnp.int32, (IRREPS, NV), 0)
    spread = jnp.where(lane // VH == irrep, jnp.broadcast_to(grouped, (IRREPS, NV)), 0.0)
    orbital = lax.broadcasted_iota(jnp.int32, (NV, VH * VH), 0) % VH
    spot = lax.broadcasted_iota(jnp.int32, (NV, VH * VH), 1)
    both = (spot // VH == orbital).astype(F32) + (spot % VH == orbital).astype(F32)
    pair[...] = exact(spread, both.astype(BF16), dims)
    new = lax.broadcasted_iota(jnp.int32, (128, VH * VH), 1)

    def rows(n, carry):
        old = lax.broadcasted_iota(jnp.int32, (128, VH * VH), 0) + n * 128
        turn[pl.ds(pl.multiple_of(n * 128, 128), 128), :] = (new == old % VH * VH + old // VH).astype(BF16)
        return carry

    lax.fori_loop(0, VH * VH // 128, rows, 0)


def exact(value, whole, dims):
    high = value.astype(BF16)
    rest = value - high.astype(F32)
    middle = rest.astype(BF16)
    low = (rest - middle.astype(F32)).astype(BF16)
    result = lax.dot_general(high, whole, dims, preferred_element_type=F32)
    result += lax.dot_general(middle, whole, dims, preferred_element_type=F32)
    return result + lax.dot_general(low, whole, dims, preferred_element_type=F32)


def relayout_kernel(rows, own, *firsts):
    def columns(k, carry):
        at = pl.ds(pl.multiple_of(k * 256, 256), 256)
        for part in range(2 * STREAMS):
            from_at = pl.ds(pl.multiple_of(k * 256 + part * RANGE, 256), 256)
            value = rows[:, :, from_at].reshape(16, 256)
            own[:, from_at] = value
            half = part % 2
            y_first, z_first = firsts[part // 2 * 2], firsts[part // 2 * 2 + 1]
            y_first[16 - 16 * half : 32 - 16 * half, at] = value
            z_first[16 * half : 16 * half + 16, at] = value
        return carry

    lax.fori_loop(0, RANGE // 256, columns, 0)


def sent_along(turn):
    near = [(1, turn - 1, 0)] if turn <= 3 else []
    return near + [(0, dy, turn - 1 - dy) for dy in range(3) if 0 <= turn - 1 - dy <= 3]


def came_along(turn):
    return [(half, dy + 1, dz) for half, dy, dz in sent_along(turn)]


def turned(blocks):
    return [(1 - half, dz, dy) for half, dy, dz in blocks]


def round_kernel(turn, y_came, z_came, y_next, z_next):
    tags = came_along(turn)
    sources = {tag: (y_came, n) for n, tag in enumerate(tags)}
    sources.update({tag: (z_came, n) for n, tag in enumerate(turned(tags))})
    wanted = sent_along(turn + 1)

    def columns(k, carry):
        at_columns = pl.ds(pl.multiple_of(k * 256, 256), 256)
        for goal, blocks in ((y_next, wanted), (z_next, turned(wanted))):
            for n, tag in enumerate(blocks):
                ref, at = sources[tag]
                goal[n * 16 : n * 16 + 16, at_columns] = ref[at * 16 : at * 16 + 16, at_columns]
        return carry

    lax.fori_loop(0, RANGE // 256, columns, 0)


def spot():
    ia, ja = lax.axis_index("ia"), lax.axis_index("ja")
    z = ia // 4 * 4 + lax.rem(ja // 2, 4)
    return lax.rem(ia, 4), ja // 8, z, lax.rem(ja, 2)


def stream_pieces(stream, refs):
    own, came = refs[0], refs[1:13]
    result = []
    for half in range(2):
        pieces = [(own, 0, 16, (stream * 2 + half) * RANGE)]
        slots = [0]
        for turn in range(1, 7):
            tags = came_along(turn)
            for ref, blocks in ((came[2 * turn - 2], tags), (came[2 * turn - 1], turned(tags))):
                for n, (which, dy, dz) in enumerate(blocks):
                    if which == half:
                        pieces.append((ref, n * 16, 16, 0))
                        slots.append(dy * 4 + dz)
        result.append((pieces, slots))
    return result


def product(stream, refs, own, partner, total, use):
    for half, (pieces, slots) in enumerate(stream_pieces(stream, refs)):
        total[...] = jnp.zeros_like(total)
        multiply(pieces, own, partner, (stream * 2 + half) * RANGE % HALF, total)
        for block, slot in enumerate(slots):
            for v in range(2):
                use(half, v, slot, total[block * 16 : block * 16 + 16, v * COLS : (v + 1) * COLS])


def stream_kernel(stream, *refs):
    own, partner = refs[13:15]
    out, total = refs[-2:]

    def use(half, v, slot, value):
        if half == 0:
            out[v, slot] = value if stream == 0 else refs[15][v, slot] + value
        else:
            out[v, slot] = out[v, slot] + value

    product(stream, refs, own, partner, total, use)


def load_kernel(part, source, held, ready):
    copies = []
    for n in range(LOADS):
        rows = pl.ds(n * (COLS // LOADS), COLS // LOADS)
        block = source.at[rows, part * HALF : (part + 1) * HALF]
        copies.append(pltpu.make_async_copy(block, held.at[rows], ready.at[n]))
    for copy in copies:
        copy.start()
    for copy in copies:
        copy.wait()


def last_stream_kernel(*refs):
    own, partner, first = refs[13:16]
    direct, crossed = refs[16:20], refs[20:24]
    total, sums = refs[24:]

    def use(half, v, slot, value):
        if half == 0:
            sums[v, slot] = first[v, slot] + value
        else:
            value = sums[v, slot] + value
            sums[v, slot] = value
            direct[slot // 4][slot % 4, v] = value

    product(STREAMS - 1, refs, own, partner, total, use)
    x, y, z, c = spot()
    for dx in range(4):
        to = lax.rem(x + dx, 4)
        for k in range(2):
            for m in range(2):
                z_low = lax.rem(to, 2) * 2 + m
                y_home = 2 * k + to // 2
                dy = lax.rem(jnp.where(c == 0, y - y_home, y_home - y) + 4, 4)
                dz = lax.rem(jnp.where(c == 0, z - z_low, z_low - z) + 8, 4)
                for core in range(2):
                    block = sums[lax.rem(c + core, 2), dy * 4 + dz]
                    a, b = block[:8], block[8:]
                    crossed[dx][k, m, core, 0] = jnp.concatenate([a[:4], b[:4]], axis=0)
                    crossed[dx][k, m, core, 1] = jnp.concatenate([a[4:], b[4:]], axis=0)


def z_pack_kernel(*refs):
    came, direct, outs, home, held = refs[:4], refs[4:8], refs[8:16], refs[16], refs[17]
    x, y, z, c = spot()
    for dx in range(4):
        held[dx] = came[dx][...]
    for dy in range(4):
        for half in range(2):
            for v in range(2):
                home[half, dy, v] = direct[dy][0, v, half * 8 : half * 8 + 8, :]
    for d in range(8):
        to = lax.rem(jnp.where(c == 0, z + d, z - d + 8), 8)
        k, x_low, side = to // 4, lax.rem(to // 2, 2), lax.rem(to, 2)
        for x_high in range(2):
            dx = lax.rem(x - (2 * x_high + x_low) + 4, 4)
            for core in range(2):
                for goal in range(2):
                    parts = []
                    for m in range(2):
                        block = held[dx, k, m, core, goal]
                        parts.append(jnp.where(side == 0, block[:4], block[4:]))
                    outs[d][x_high * 2 + goal, core] = jnp.concatenate(parts, axis=0)
        if d > 4:
            for half in range(2):
                for dy in range(4):
                    for v in range(2):
                        value = direct[dy][8 - d, v, half * 8 : half * 8 + 8, :]
                        outs[d][4 + half * 4 + dy, v] = value


def y_pack_kernel(*refs):
    came, outs, held = refs[:8], refs[8:12], refs[12]
    for d in range(8):
        held[d] = came[d][:4]
    x, y, z, c = spot()
    for e in range(4):
        to = lax.rem(y + e, 4)
        z_high, x_high = to // 2, lax.rem(to, 2)
        for z_low in range(4):
            froms = []
            for m in range(2):
                low = lax.rem(x, 2) * 2 + m
                up = lax.rem(z_high * 4 + low + lax.rem(z_low - low + 4, 4), 8)
                down = lax.rem(z_high * 4 + low - lax.rem(low - z_low + 4, 4) + 8, 8)
                froms.append(lax.rem(jnp.where(c == 0, z - up, down - z) + 8, 8))
            for goal in range(2):
                for core in range(2):
                    a = held[froms[0], x_high * 2 + goal, core]
                    b = held[froms[1], x_high * 2 + goal, core]
                    outs[e][z_low, goal, core] = jnp.concatenate([a[:4], b[4:]], axis=0)


def swap_pack_kernel(*refs):
    c = spot()[3]
    for e in range(4):
        for z_low in range(4):
            refs[4][e, z_low] = refs[e][z_low, 1 - c]


def base_kernel(*refs):
    came, home, r_ref, base, held = refs[:3], refs[3], refs[4], refs[5], refs[6]
    x, y, z, c = spot()
    for half in range(2):
        held[half, 0] = home[half]
        for dz in range(1, 4):
            held[half, dz] = came[3 - dz][4 + half * 4 : 8 + half * 4]
    for dy in range(4):
        source = lax.rem(jnp.where(c == 0, y + dy, y - dy + 4), 4)
        for z_low in range(4):
            dz = lax.rem(jnp.where(c == 0, z_low - z, z - z_low) + 8, 4)
            for core in range(2):
                v = lax.rem(c + core, 2)
                at = pl.ds(pl.multiple_of(source * 2048 + z_low * 512 + core * COLS, COLS), COLS)
                straight = jnp.concatenate([held[0, dz, dy, v], held[1, dz, dy, v]], axis=0)
                base[:, at] = r_ref[:, :, at].reshape(16, COLS) + straight


def final_kernel(*refs):
    mirror, swapped = refs[:4], refs[4]
    t_ref, base, pair, occupied, turn, residual, updated, moved_ref, turned_ref = refs[5:]
    x, y, z, c = spot()
    lane = lax.broadcasted_iota(jnp.int32, (16, 64), 1)
    row = lax.broadcasted_iota(jnp.int32, (16, 64), 0)
    i = (z // 4 * 4 + x) * 8 + row // 2
    j = ((y * 4 + lax.rem(z, 4)) * 2 + c) * 2 + row % 2
    first = jnp.sum(jnp.where(lane == i, occupied[...], 0.0), axis=1, keepdims=True)
    second = jnp.sum(jnp.where(lane == j, occupied[...], 0.0), axis=1, keepdims=True)
    order = (0, 2, 1, 3)
    for e in range(4):
        for z_low in range(4):
            for core in range(2):
                kept, given = mirror[e][z_low, c, core], swapped[e, z_low, core]
                a, b = jnp.where(c == 0, kept, given), jnp.where(c == 0, given, kept)
                rows = [s[m * 4 + n : m * 4 + n + 1] for m in range(2) for s in (a, b) for n in order]
                column = (z_low % 2 * 2 + core) * COLS
                group = e * 2 + z_low // 2
                moved_ref[group * 16 : group * 16 + 16, column : column + COLS] = jnp.concatenate(rows, axis=0)
    value = moved_ref[...]

    def columns(n, carry):
        at = pl.ds(pl.multiple_of(n * 256, 256), 256)
        turned_ref[:, at] = exact(value, turn[:, at], (((1,), (0,)), ((), ())))
        return carry

    lax.fori_loop(0, VH * VH // 256, columns, 0)
    for e in range(4):
        source = lax.rem(y - e + 4, 4)
        for half in range(2):
            group = e * 2 + half
            at = pl.ds(pl.multiple_of(source * 2048 + half * 1024, 1024), 1024)
            total = base[:, at] + turned_ref[group * 16 : group * 16 + 16, :]
            residual[:, :, at] = total.reshape(8, 2, 1024)
            ratio = total / (pair[pl.ds(source * 2 + half, 1), :] - first - second)
            updated[:, :, at] = t_ref[:, :, at] + ratio.reshape(8, 2, 1024)


VMEM = pl.BlockSpec(memory_space=pltpu.VMEM)


def shape(*dims):
    return jax.ShapeDtypeStruct(dims, F32)


def call(kernel, name, operands, outs, scratch=(), limit=8, cost=None):
    return pl.pallas_call(
        kernel,
        in_specs=[VMEM] * len(operands),
        out_specs=[VMEM] * len(outs),
        out_shape=[shape(*dims) if isinstance(dims, tuple) else dims for dims in outs],
        scratch_shapes=[pltpu.VMEM(dims, F32) for dims in scratch],
        compiler_params=pltpu.CompilerParams(vmem_limit_bytes=limit * 1024 * 1024),
        cost_estimate=cost,
        name=name,
    )(*operands)


def load(array, part):
    return pl.pallas_call(
        lambda *refs: load_kernel(part, *refs),
        in_specs=[pl.BlockSpec(memory_space=pltpu.HBM)],
        out_specs=VMEM,
        out_shape=shape(COLS, HALF),
        scratch_shapes=[pltpu.SemaphoreType.DMA((LOADS,))],
        compiler_params=pltpu.CompilerParams(vmem_limit_bytes=1024 * 1024),
        cost_estimate=pl.CostEstimate(flops=0, bytes_accessed=8 << 20, transcendentals=0),
        name="load",
    )(array)


def shards(amplitudes, residual_in, ladder_ints, occ_energy, virt_energy, virt_order):
    own, *firsts = call(
        relayout_kernel, "relayout", [amplitudes], [(16, NP)] + [(32, RANGE)] * (2 * STREAMS)
    )
    pair_energy, turn_matrix = call(
        prepare_kernel,
        "prepare",
        [virt_order.reshape(1, NV), virt_energy.reshape(1, NV)],
        [(IRREPS, VH * VH), jax.ShapeDtypeStruct((VH * VH, VH * VH), BF16)],
        limit=16,
    )

    y_next, z_next = firsts[::2], firsts[1::2]
    arrived, loaded, pending = [[] for _ in range(STREAMS)], [], None
    partner = shift(ladder_ints, dc=1)
    for turn in range(1, 7):
        for stream in range(STREAMS):
            y_came = shift(y_next[stream], dy=1, way=1)
            z_came = shift(z_next[stream], dz=1, way=1)
            arrived[stream] += [y_came, z_came]
            if turn < 6:
                rows = len(sent_along(turn + 1)) * 16
                y_next[stream], z_next[stream] = call(
                    lambda *refs, turn=turn: round_kernel(turn, *refs),
                    "round",
                    [y_came, z_came],
                    [(rows, RANGE)] * 2,
                )
            if turn == 4 and stream == 0:
                y_next[0], pair_energy, turn_matrix = lax.optimization_barrier(
                    (y_next[0], pair_energy, turn_matrix)
                )
            if turn < 6 and stream == 0 and pending is not None:
                y_next[0], pending = lax.optimization_barrier((y_next[0], pending))
                loaded.append(pending)
            if turn < 5 and stream == STREAMS - 1:
                n = turn - 1
                source = lax.optimization_barrier(((ladder_ints, partner)[n % 2], y_came))[0]
                pending = load(source, n // 2)

    cost = pl.CostEstimate(flops=2 * 3 * ROWS * 2 * COLS * 2 * RANGE, bytes_accessed=6 << 20, transcendentals=0)
    sums = (2, 16, 16, COLS)
    total = (ROWS, 2 * COLS)
    first = []
    for stream in range(STREAMS - 1):
        held = stream * 2 * RANGE // HALF * 2
        first = list(call(
            lambda *refs, stream=stream: stream_kernel(stream, *refs),
            "stream",
            [own] + arrived[stream] + loaded[held : held + 2] + first,
            [sums],
            [total],
            limit=MULTIPLY_LIMIT,
            cost=cost,
        ))
    results = call(
        last_stream_kernel,
        "last_stream",
        [own] + arrived[STREAMS - 1] + loaded[2:] + first,
        [(4, 2, 16, COLS)] * 4 + [(2, 2, 2, 2, 8, COLS)] * 4,
        [total, sums],
        limit=MULTIPLY_LIMIT,
        cost=cost,
    )

    direct, crossed = results[:4], results[4:]
    came = [crossed[0]] + [shift(crossed[dx], dx=dx) for dx in range(1, 4)]
    direct = [direct[0]] + [shift(direct[dy], dy=-dy, way=1) for dy in range(1, 4)]
    chunk, mixed = (4, 2, 8, COLS), (12, 2, 8, COLS)
    *z_sent, home = call(
        z_pack_kernel,
        "z_pack",
        came + direct,
        [mixed if d > 4 else chunk for d in range(8)] + [(2, 4, 2, 8, COLS)],
        [(4, 2, 2, 2, 2, 8, COLS)],
    )
    z_came = [z_sent[0]] + [shift(z_sent[d], dz=d, way=1) for d in range(1, 8)]
    y_sent = call(y_pack_kernel, "y_pack", z_came, [(4, 2, 2, 8, COLS)] * 4, [(8,) + chunk])
    mirror = [y_sent[0]] + [shift(y_sent[e], dy=e) for e in range(1, 4)]
    straight = z_came[5:]
    (base,) = call(base_kernel, "base", straight + [home, residual_in], [(16, NP)], [(2, 4) + chunk])
    (swapped,) = call(swap_pack_kernel, "swap_pack", mirror, [(4, 4, 2, 8, COLS)])
    swapped = shift(swapped, dc=1)
    residual, updated = call(
        final_kernel,
        "final",
        mirror + [swapped, amplitudes, base, pair_energy, occ_energy.reshape(1, 64), turn_matrix],
        [(8, 2, NP)] * 2,
        [(128, VH * VH)] * 2,
    )
    return residual, updated


def solution(mesh):
    placed = (P("ia", "ja", None), P("ia", "ja", None), P("ja", None), P(), P(), P())
    return jax.shard_map(
        shards,
        mesh=mesh,
        in_specs=placed,
        out_specs=(P("ia", "ja", None), P("ia", "ja", None)),
        check_vma=False,
    )
```

profile of v0, /device:TPU:1, one launch (start us, length us, event | category | flops | bytes accessed | tf_op | source)
XLA Modules:
  0.0 127.9 jit_solution(5389736666354229716)
XLA Ops:
  0.6 3.3 %collective-permute-start.18 = (f32[256,8192]{1,0:T(8,128)}, f32[256,8192]{1,0:T(8,128)S(1)}, u32[]{:S(2)}, u32[]{:S(2)}) collective-permute-start(f32[256,8192]{1,0:T(8,128)} %refs_0_.1), channel_id=1, source_target_pairs={{0,1},{1,0},{2,3},{3,2},{4,5},{5,4},{6,7},{7,6},{128,129},{129,128... | collective-permute-start | bytes 25165832 | tf_op jit(solution)/shard_map/ppermute | solution.py:43
  4.0 1.0 copy-done.1
  5.0 0.2 relayout.1
  5.2 1.1 collective-permute-start.12
  6.3 5.6 %collective-permute-start.13 = (f32[32,2048]{1,0:T(8,128)S(1)}, f32[32,2048]{1,0:T(8,128)S(1)}, u32[]{:S(2)}, u32[]{:S(2)}) collective-permute-start(f32[32,2048]{1,0:T(8,128)S(1)} %get-tuple-element.79), channel_id=1, source_target_pairs={{0,2},{1,135},{2,4},{3,1},{4,6},{5,3},{6,128},{7,5},{128,130},{129... | collective-permute-start | bytes 786440 | tf_op jit(solution)/shard_map/ppermute | solution.py:43
  11.9 0.5 collective-permute-start
  12.3 0.7 collective-permute-start.1
  13.1 2.1 %collective-permute-done.13.refs_1_.refs_2_ = f32[32,2048]{1,0:T(8,128)S(1)} collective-permute-done((f32[32,2048]{1,0:T(8,128)S(1)}, f32[32,2048]{1,0:T(8,128)S(1)}, u32[]{:S(2)}, u32[]{:S(2)}) %collective-permute-start.13) | collective-permute-done | bytes 262176 | tf_op jit(solution)/shard_map/ppermute | solution.py:43
  15.2 0.5 collective-permute-start.14
  15.8 3.1 %collective-permute-start.15 = (f32[48,2048]{1,0:T(8,128)S(1)}, f32[48,2048]{1,0:T(8,128)S(1)}, u32[]{:S(2)}, u32[]{:S(2)}) collective-permute-start(f32[48,2048]{1,0:T(8,128)S(1)} %get-tuple-element.81), channel_id=1, source_target_pairs={{0,2},{1,135},{2,4},{3,1},{4,6},{5,3},{6,128},{7,5},{128,130},{129... | collective-permute-start | bytes 1179656 | tf_op jit(solution)/shard_map/ppermute | solution.py:43
  19.0 0.2 collective-permute-start.2
  19.2 2.5 %collective-permute-start.3 = (f32[48,2048]{1,0:T(8,128)S(1)}, f32[48,2048]{1,0:T(8,128)S(1)}, u32[]{:S(2)}, u32[]{:S(2)}) collective-permute-start(f32[48,2048]{1,0:T(8,128)S(1)} %get-tuple-element.69), channel_id=1, source_target_pairs={{0,2},{1,135},{2,4},{3,1},{4,6},{5,3},{6,128},{7,5},{128,130},{129... | collective-permute-start | bytes 1179656 | tf_op jit(solution)/shard_map/ppermute | solution.py:43
  21.7 3.4 %copy-done = f32[256,8192]{1,0:T(8,128)S(1)} copy-done((f32[256,8192]{1,0:T(8,128)S(1)}, f32[256,8192]{1,0:T(8,128)}, u32[]{:S(2)}) %copy-start) | copy-done | bytes 8388632
  25.1 0.3 load.4.refs_13_
  25.5 0.2 collective-permute-start.16
  25.8 1.5 %collective-permute-start.17 = (f32[64,2048]{1,0:T(8,128)S(1)}, f32[64,2048]{1,0:T(8,128)S(1)}, u32[]{:S(2)}, u32[]{:S(2)}) collective-permute-start(f32[64,2048]{1,0:T(8,128)S(1)} %get-tuple-element.85), channel_id=1, source_target_pairs={{0,2},{1,135},{2,4},{3,1},{4,6},{5,3},{6,128},{7,5},{128,130},{129... | collective-permute-start | bytes 1572872 | tf_op jit(solution)/shard_map/ppermute | solution.py:43
  27.3 0.5 collective-permute-done.3.refs_1_.refs_4_
  27.9 0.4 collective-permute-start.4
  28.3 3.2 %collective-permute-start.5 = (f32[64,2048]{1,0:T(8,128)S(1)}, f32[64,2048]{1,0:T(8,128)S(1)}, u32[]{:S(2)}, u32[]{:S(2)}) collective-permute-start(f32[64,2048]{1,0:T(8,128)S(1)} %get-tuple-element.71), channel_id=1, source_target_pairs={{0,2},{1,135},{2,4},{3,1},{4,6},{5,3},{6,128},{7,5},{128,130},{129... | collective-permute-start | bytes 1572872 | tf_op jit(solution)/shard_map/ppermute | solution.py:43
  31.5 2.4 %collective-permute-done.16.refs_0_.refs_5_ = f32[64,2048]{1,0:T(8,128)S(1)} collective-permute-done((f32[64,2048]{1,0:T(8,128)S(1)}, f32[64,2048]{1,0:T(8,128)S(1)}, u32[]{:S(2)}, u32[]{:S(2)}) %collective-permute-start.16) | collective-permute-done | bytes 524320 | tf_op jit(solution)/shard_map/ppermute | solution.py:43
  34.2 2.8 %collective-permute-start.20 = (f32[48,2048]{1,0:T(8,128)S(1)}, f32[48,2048]{1,0:T(8,128)S(1)}, u32[]{:S(2)}, u32[]{:S(2)}) collective-permute-start(f32[48,2048]{1,0:T(8,128)S(1)} %get-tuple-element.89), channel_id=1, source_target_pairs={{0,2},{1,135},{2,4},{3,1},{4,6},{5,3},{6,128},{7,5},{128,130},{129... | collective-permute-start | bytes 1179656 | tf_op jit(solution)/shard_map/ppermute | solution.py:43
  37.1 0.3 load.5.refs_14_
  37.5 2.1 %collective-permute-done.4.refs_0_.refs_5_ = f32[64,2048]{1,0:T(8,128)S(1)} collective-permute-done((f32[64,2048]{1,0:T(8,128)S(1)}, f32[64,2048]{1,0:T(8,128)S(1)}, u32[]{:S(2)}, u32[]{:S(2)}) %collective-permute-start.4) | collective-permute-done | bytes 524320 | tf_op jit(solution)/shard_map/ppermute | solution.py:43
  39.8 1.5 %collective-permute-start.6 = (f32[48,2048]{1,0:T(8,128)S(1)}, f32[48,2048]{1,0:T(8,128)S(1)}, u32[]{:S(2)}, u32[]{:S(2)}) collective-permute-start(f32[48,2048]{1,0:T(8,128)S(1)} %get-tuple-element.72), channel_id=1, source_target_pairs={{0,8},{1,25},{2,10},{3,27},{4,12},{5,29},{6,14},{7,31},{128,136},{... | collective-permute-start | bytes 1179656 | tf_op jit(solution)/shard_map/ppermute | solution.py:43
  41.3 1.5 %collective-permute-start.7 = (f32[48,2048]{1,0:T(8,128)S(1)}, f32[48,2048]{1,0:T(8,128)S(1)}, u32[]{:S(2)}, u32[]{:S(2)}) collective-permute-start(f32[48,2048]{1,0:T(8,128)S(1)} %get-tuple-element.73), channel_id=1, source_target_pairs={{0,2},{1,135},{2,4},{3,1},{4,6},{5,3},{6,128},{7,5},{128,130},{129... | collective-permute-start | bytes 1179656 | tf_op jit(solution)/shard_map/ppermute | solution.py:43
  42.8 1.5 %prepare.1 = (f32[8,1024]{1,0:T(8,128)S(1)}, bf16[1024,1024]{1,0:T(8,128)(2,1)S(1)}) custom-call(s32[1,256]{1,0:T(1,128)S(1)} %bitcast.5, f32[1,256]{1,0:T(1,128)S(1)} %bitcast.6), custom_call_target="tpu_custom_call" | custom-call | tf_op jit(solution)/shard_map/prepare/pallas_call | solution.py:359
  44.3 0.3 load.6.refs_13_
  44.8 2.8 %collective-permute-start.21 = (f32[32,2048]{1,0:T(8,128)S(1)}, f32[32,2048]{1,0:T(8,128)S(1)}, u32[]{:S(2)}, u32[]{:S(2)}) collective-permute-start(f32[32,2048]{1,0:T(8,128)S(1)} %get-tuple-element.96), channel_id=1, source_target_pairs={{0,8},{1,25},{2,10},{3,27},{4,12},{5,29},{6,14},{7,31},{128,136},{... | collective-permute-start | bytes 786440 | tf_op jit(solution)/shard_map/ppermute | solution.py:43
  47.5 1.1 collective-permute-done.6.refs_0_.refs_7_
  48.7 1.7 %collective-permute-start.8 = (f32[32,2048]{1,0:T(8,128)S(1)}, f32[32,2048]{1,0:T(8,128)S(1)}, u32[]{:S(2)}, u32[]{:S(2)}) collective-permute-start(f32[32,2048]{1,0:T(8,128)S(1)} %get-tuple-element.74), channel_id=1, source_target_pairs={{0,8},{1,25},{2,10},{3,27},{4,12},{5,29},{6,14},{7,31},{128,136},{... | collective-permute-start | bytes 786440 | tf_op jit(solution)/shard_map/ppermute | solution.py:43
  50.3 3.1 %collective-permute-start.9 = (f32[32,2048]{1,0:T(8,128)S(1)}, f32[32,2048]{1,0:T(8,128)S(1)}, u32[]{:S(2)}, u32[]{:S(2)}) collective-permute-start(f32[32,2048]{1,0:T(8,128)S(1)} %get-tuple-element.75), channel_id=1, source_target_pairs={{0,2},{1,135},{2,4},{3,1},{4,6},{5,3},{6,128},{7,5},{128,130},{129... | collective-permute-start | bytes 786440 | tf_op jit(solution)/shard_map/ppermute | solution.py:43
  53.4 0.3 load.7.refs_14_
  53.9 0.5 collective-permute-start.23
  54.4 1.8 %collective-permute-start.24 = (f32[16,2048]{1,0:T(8,128)S(1)}, f32[16,2048]{1,0:T(8,128)S(1)}, u32[]{:S(2)}, u32[]{:S(2)}) collective-permute-start(f32[16,2048]{1,0:T(8,128)S(1)} %get-tuple-element.102), channel_id=1, source_target_pairs={{0,2},{1,135},{2,4},{3,1},{4,6},{5,3},{6,128},{7,5},{128,130},{129... | collective-permute-start | bytes 393224 | tf_op jit(solution)/shard_map/ppermute | solution.py:43
  56.2 0.5 collective-permute-done.9.refs_1_.refs_10_
  56.8 0.5 collective-permute-start.10
  57.3 3.1 %collective-permute-start.11 = (f32[16,2048]{1,0:T(8,128)S(1)}, f32[16,2048]{1,0:T(8,128)S(1)}, u32[]{:S(2)}, u32[]{:S(2)}) collective-permute-start(f32[16,2048]{1,0:T(8,128)S(1)} %get-tuple-element.77), channel_id=1, source_target_pairs={{0,2},{1,135},{2,4},{3,1},{4,6},{5,3},{6,128},{7,5},{128,130},{129... | collective-permute-start | bytes 393224 | tf_op jit(solution)/shard_map/ppermute | solution.py:43
  60.5 5.2 %stream.1.refs_15_ = f32[2,16,16,256]{3,2,1,0:T(8,128)S(1)} custom-call(f32[16,8192]{1,0:T(8,128)S(1)} %get-tuple-element.65.refs_0_, f32[32,2048]{1,0:T(8,128)S(1)} %collective-permute-done.12.refs_0_.refs_1_, f32[32,2048]{1,0:T(8,128)S(1)} %collective-permute-done.13.refs_1_.refs_2_, f32[48,2048]{1,0:T(8,128)S(1)} %collective-permute-done.14.refs_0_.refs_3_, ...), custom_call_target="tpu_custom_call" | custom-call | flops 3221225472 | bytes 6291456 | tf_op jit(solution)/shard_map/stream/pallas_call | solution.py:359
  65.7 5.3 %last_stream.1 = (f32[4,2,16,256]{3,2,1,0:T(8,128)S(1)}, f32[4,2,16,256]{3,2,1,0:T(8,128)S(1)}, f32[4,2,16,256]{3,2,1,0:T(8,128)S(1)}, f32[4,2,16,256]{3,2,1,0:T...) custom-call(f32[16,8192]{1,0:T(8,128)S(1)} %get-tuple-element.65.ref, ...), custom_call_target="tpu_custom_call" | custom-call | flops 3221225472 | bytes 6291456 | tf_op jit(solution)/shard_map/last_stream/pallas_call | solution.py:359
  71.0 1.3 %collective-permute-start.25 = (f32[2,2,2,2,8,256]{5,4,3,2,1,0:T(8,128)S(1)}, f32[2,2,2,2,8,256]{5,4,3,2,1,0:T(8,128)S(1)}, u32[]{:S(2)}, u32[]{:S(2)}) collective-permute-start(f32[2,2,2,2,8,256]{5,4,3,2,1,0:T(8,128)S(1)} %get-tuple-element.106), channel_id=1, source_target_pairs={{0,32},{1,33},{2,34},{3,35},{4,36},{5,37},{6,38},{7,39},{128,160},... | collective-permute-start | bytes 393224 | tf_op jit(solution)/shard_map/ppermute | solution.py:43
  72.3 2.5 %collective-permute-start.26 = (f32[2,2,2,2,8,256]{5,4,3,2,1,0:T(8,128)S(1)}, f32[2,2,2,2,8,256]{5,4,3,2,1,0:T(8,128)S(1)}, u32[]{:S(2)}, u32[]{:S(2)}) collective-permute-start(f32[2,2,2,2,8,256]{5,4,3,2,1,0:T(8,128)S(1)} %get-tuple-element.107), channel_id=1, source_target_pairs={{0,64},{1,65},{2,66},{3,67},{4,68},{5,69},{6,70},{7,71},{128,192},... | collective-permute-start | bytes 393224 | tf_op jit(solution)/shard_map/ppermute | solution.py:43
  74.8 1.1 collective-permute-start.27
  75.9 1.3 %collective-permute-start.28 = (f32[4,2,16,256]{3,2,1,0:T(8,128)S(1)}, f32[4,2,16,256]{3,2,1,0:T(8,128)S(1)}, u32[]{:S(2)}, u32[]{:S(2)}) collective-permute-start(f32[4,2,16,256]{3,2,1,0:T(8,128)S(1)} %get-tuple-element.110), channel_id=1, source_target_pairs={{0,24},{1,9},{2,26},{3,11},{4,28},{5,13},{6,30},{7,15},{128,152},{... | collective-permute-start | bytes 393224 | tf_op jit(solution)/shard_map/ppermute | solution.py:43
  77.4 2.2 %collective-permute-start.30 = (f32[4,2,16,256]{3,2,1,0:T(8,128)S(1)}, f32[4,2,16,256]{3,2,1,0:T(8,128)S(1)}, u32[]{:S(2)}, u32[]{:S(2)}) collective-permute-start(f32[4,2,16,256]{3,2,1,0:T(8,128)S(1)} %get-tuple-element.112), channel_id=1, source_target_pairs={{0,8},{1,25},{2,10},{3,27},{4,12},{5,29},{6,14},{7,31},{128,136},{... | collective-permute-start | bytes 393224 | tf_op jit(solution)/shard_map/ppermute | solution.py:43
  79.6 1.6 %collective-permute-done.28.refs_5_ = f32[4,2,16,256]{3,2,1,0:T(8,128)S(1)} collective-permute-done((f32[4,2,16,256]{3,2,1,0:T(8,128)S(1)}, f32[4,2,16,256]{3,2,1,0:T(8,128)S(1)}, u32[]{:S(2)}, u32[]{:S(2)}) %collective-permute-start.28) | collective-permute-done | bytes 131104 | tf_op jit(solution)/shard_map/ppermute | solution.py:43
  81.2 1.6 %collective-permute-done.29.refs_6_ = f32[4,2,16,256]{3,2,1,0:T(8,128)S(1)} collective-permute-done((f32[4,2,16,256]{3,2,1,0:T(8,128)S(1)}, f32[4,2,16,256]{3,2,1,0:T(8,128)S(1)}, u32[]{:S(2)}, u32[]{:S(2)}) %collective-permute-start.29) | collective-permute-done | bytes 131104 | tf_op jit(solution)/shard_map/ppermute | solution.py:43
  82.8 0.4 collective-permute-done.30.refs_7_
  83.7 1.9 %collective-permute-start.37 = (f32[12,2,8,256]{3,2,1,0:T(8,128)S(1)}, f32[12,2,8,256]{3,2,1,0:T(8,128)S(1)}, u32[]{:S(2)}, u32[]{:S(2)}) collective-permute-start(f32[12,2,8,256]{3,2,1,0:T(8,128)S(1)} %get-tuple-element.120), channel_id=1, source_target_pairs={{0,134},{1,3},{2,0},{3,5},{4,2},{5,7},{6,4},{7,129},{128,6},{129,1... | collective-permute-start | bytes 589832 | tf_op jit(solution)/shard_map/ppermute | solution.py:43
  85.5 1.9 %collective-permute-start.31 = (f32[4,2,8,256]{3,2,1,0:T(8,128)S(1)}, f32[4,2,8,256]{3,2,1,0:T(8,128)S(1)}, u32[]{:S(2)}, u32[]{:S(2)}) collective-permute-start(f32[4,2,8,256]{3,2,1,0:T(8,128)S(1)} %get-tuple-element.114), channel_id=1, source_target_pairs={{0,2},{1,135},{2,4},{3,1},{4,6},{5,3},{6,128},{7,5},{128,130},{129... | collective-permute-start | bytes 196616 | tf_op jit(solution)/shard_map/ppermute | solution.py:43
  87.5 1.2 collective-permute-start.32
  88.7 1.2 collective-permute-done.31.refs_1_
  89.9 3.2 %collective-permute-start.33 = (f32[4,2,8,256]{3,2,1,0:T(8,128)S(1)}, f32[4,2,8,256]{3,2,1,0:T(8,128)S(1)}, u32[]{:S(2)}, u32[]{:S(2)}) collective-permute-start(f32[4,2,8,256]{3,2,1,0:T(8,128)S(1)} %get-tuple-element.116), channel_id=1, source_target_pairs={{0,6},{1,131},{2,128},{3,133},{4,130},{5,135},{6,132},{7,1},{128,1... | collective-permute-start | bytes 196616 | tf_op jit(solution)/shard_map/ppermute | solution.py:43
  93.0 2.6 %collective-permute-start.34 = (f32[4,2,8,256]{3,2,1,0:T(8,128)S(1)}, f32[4,2,8,256]{3,2,1,0:T(8,128)S(1)}, u32[]{:S(2)}, u32[]{:S(2)}) collective-permute-start(f32[4,2,8,256]{3,2,1,0:T(8,128)S(1)} %get-tuple-element.117), channel_id=1, source_target_pairs={{0,128},{1,129},{2,130},{3,131},{4,132},{5,133},{6,134},{7,135},{1... | collective-permute-start | bytes 196616 | tf_op jit(solution)/shard_map/ppermute | solution.py:43
  95.6 0.4 collective-permute-done.33.refs_3_
  96.1 5.0 %collective-permute-done.34.refs_4_ = f32[4,2,8,256]{3,2,1,0:T(8,128)S(1)} collective-permute-done((f32[4,2,8,256]{3,2,1,0:T(8,128)S(1)}, f32[4,2,8,256]{3,2,1,0:T(8,128)S(1)}, u32[]{:S(2)}, u32[]{:S(2)}) %collective-permute-start.34) | collective-permute-done | bytes 65568 | tf_op jit(solution)/shard_map/ppermute | solution.py:43
  101.1 0.3 y_pack.1
  101.6 3.9 %collective-permute-start.39 = (f32[4,2,2,8,256]{4,3,2,1,0:T(8,128)S(1)}, f32[4,2,2,8,256]{4,3,2,1,0:T(8,128)S(1)}, u32[]{:S(2)}, u32[]{:S(2)}) collective-permute-start(f32[4,2,2,8,256]{4,3,2,1,0:T(8,128)S(1)} %get-tuple-element.123), channel_id=1, source_target_pairs={{0,16},{1,17},{2,18},{3,19},{4,20},{5,21},{6,22},{7,23},{128,144},... | collective-permute-start | bytes 393224 | tf_op jit(solution)/shard_map/ppermute | solution.py:43
  105.5 1.3 %collective-permute-done.38.refs_1_ = f32[4,2,2,8,256]{4,3,2,1,0:T(8,128)S(1)} collective-permute-done((f32[4,2,2,8,256]{4,3,2,1,0:T(8,128)S(1)}, f32[4,2,2,8,256]{4,3,2,1,0:T(8,128)S(1)}, u32[]{:S(2)}, u32[]{:S(2)}) %collective-permute-start.38) | collective-permute-done | bytes 131104 | tf_op jit(solution)/shard_map/ppermute | solution.py:43
  106.8 2.4 %collective-permute-done.39.refs_2_ = f32[4,2,2,8,256]{4,3,2,1,0:T(8,128)S(1)} collective-permute-done((f32[4,2,2,8,256]{4,3,2,1,0:T(8,128)S(1)}, f32[4,2,2,8,256]{4,3,2,1,0:T(8,128)S(1)}, u32[]{:S(2)}, u32[]{:S(2)}) %collective-permute-start.39) | collective-permute-done | bytes 131104 | tf_op jit(solution)/shard_map/ppermute | solution.py:43
  109.3 0.4 collective-permute-done.40.refs_3_
  109.7 14.0 %collective-permute-start.41 = (f32[4,4,2,8,256]{4,3,2,1,0:T(8,128)S(1)}, f32[4,4,2,8,256]{4,3,2,1,0:T(8,128)S(1)}, u32[]{:S(2)}, u32[]{:S(2)}) collective-permute-start(f32[4,4,2,8,256]{4,3,2,1,0:T(8,128)S(1)} %swap_pack.1), channel_id=1, source_target_pairs={{0,1},{1,0},{2,3},{3,2},{4,5},{5,4},{6,7},{7,6},{128,129},{129,128... | collective-permute-start | bytes 786440 | tf_op jit(solution)/shard_map/ppermute | solution.py:43
  123.7 0.2 base.1.refs_6_
  123.9 0.9 collective-permute-done.41.refs_4_
  124.9 3.0 %final.1 = (f32[8,2,8192]{2,1,0:T(2,128)}, f32[8,2,8192]{2,1,0:T(2,128)}) custom-call(f32[4,2,2,8,256]{4,3,2,1,0:T(8,128)S(1)} %get-tuple-element.121.refs_0_, f32[4,2,2,8,256]{4,3,2,1,0:T(8,128)S(1)} %collective-permute-done.38.refs_1_, f32[4,2,2,8,256]{4,3,2,1,0:T(8,128)S(1)} %collective-permute-done.39.refs_2_, ...), custom_call_target="tpu_custom_call" | custom-call | tf_op jit(solution)/shard_map/final/pallas_call | solution.py:359
  (62 shorter events, 2.0 us)
Async XLA Ops:
  0.6 36.4 %collective-permute-start.18 = (f32[256,8192]{1,0:T(8,128)}, f32[256,8192]{1,0:T(8,128)S(1)}, u32[]{:S(2)}, u32[]{:S(2)}) collective-permute-start(f32[256,8192]{1,0:T(8,128)} %refs_0_.1), channel_id=1, source_target_pairs={{0,1},{1,0},{2,3},{3,2},{4,5},{5,4},{6,7},{7,6},{128,129},{129,128... | collective-permute-start | bytes 25165832 | tf_op jit(solution)/shard_map/ppermute | solution.py:43
  4.0 1.0 copy-start.1
  5.2 7.8 %collective-permute-start.12 = (f32[32,2048]{1,0:T(8,128)S(1)}, f32[32,2048]{1,0:T(8,128)S(1)}, u32[]{:S(2)}, u32[]{:S(2)}) collective-permute-start(f32[32,2048]{1,0:T(8,128)S(1)} %get-tuple-element.78), channel_id=1, source_target_pairs={{0,8},{1,25},{2,10},{3,27},{4,12},{5,29},{6,14},{7,31},{128,136},{... | collective-permute-start | bytes 786440 | tf_op jit(solution)/shard_map/ppermute | solution.py:43
  6.3 8.9 %collective-permute-start.13 = (f32[32,2048]{1,0:T(8,128)S(1)}, f32[32,2048]{1,0:T(8,128)S(1)}, u32[]{:S(2)}, u32[]{:S(2)}) collective-permute-start(f32[32,2048]{1,0:T(8,128)S(1)} %get-tuple-element.79), channel_id=1, source_target_pairs={{0,2},{1,135},{2,4},{3,1},{4,6},{5,3},{6,128},{7,5},{128,130},{129... | collective-permute-start | bytes 786440 | tf_op jit(solution)/shard_map/ppermute | solution.py:43
  11.9 7.0 %collective-permute-start = (f32[32,2048]{1,0:T(8,128)S(1)}, f32[32,2048]{1,0:T(8,128)S(1)}, u32[]{:S(2)}, u32[]{:S(2)}) collective-permute-start(f32[32,2048]{1,0:T(8,128)S(1)} %get-tuple-element.66), channel_id=1, source_target_pairs={{0,8},{1,25},{2,10},{3,27},{4,12},{5,29},{6,14},{7,31},{128,136},{... | collective-permute-start | bytes 786440 | tf_op jit(solution)/shard_map/ppermute | solution.py:43
  12.3 6.6 %collective-permute-start.1 = (f32[32,2048]{1,0:T(8,128)S(1)}, f32[32,2048]{1,0:T(8,128)S(1)}, u32[]{:S(2)}, u32[]{:S(2)}) collective-permute-start(f32[32,2048]{1,0:T(8,128)S(1)} %get-tuple-element.67), channel_id=1, source_target_pairs={{0,2},{1,135},{2,4},{3,1},{4,6},{5,3},{6,128},{7,5},{128,130},{129... | collective-permute-start | bytes 786440 | tf_op jit(solution)/shard_map/ppermute | solution.py:43
  15.2 10.2 %collective-permute-start.14 = (f32[48,2048]{1,0:T(8,128)S(1)}, f32[48,2048]{1,0:T(8,128)S(1)}, u32[]{:S(2)}, u32[]{:S(2)}) collective-permute-start(f32[48,2048]{1,0:T(8,128)S(1)} %get-tuple-element.80), channel_id=1, source_target_pairs={{0,8},{1,25},{2,10},{3,27},{4,12},{5,29},{6,14},{7,31},{128,136},{... | collective-permute-start | bytes 1179656 | tf_op jit(solution)/shard_map/ppermute | solution.py:43
  15.8 9.7 %collective-permute-start.15 = (f32[48,2048]{1,0:T(8,128)S(1)}, f32[48,2048]{1,0:T(8,128)S(1)}, u32[]{:S(2)}, u32[]{:S(2)}) collective-permute-start(f32[48,2048]{1,0:T(8,128)S(1)} %get-tuple-element.81), channel_id=1, source_target_pairs={{0,2},{1,135},{2,4},{3,1},{4,6},{5,3},{6,128},{7,5},{128,130},{129... | collective-permute-start | bytes 1179656 | tf_op jit(solution)/shard_map/ppermute | solution.py:43
  19.0 8.3 %collective-permute-start.2 = (f32[48,2048]{1,0:T(8,128)S(1)}, f32[48,2048]{1,0:T(8,128)S(1)}, u32[]{:S(2)}, u32[]{:S(2)}) collective-permute-start(f32[48,2048]{1,0:T(8,128)S(1)} %get-tuple-element.68), channel_id=1, source_target_pairs={{0,8},{1,25},{2,10},{3,27},{4,12},{5,29},{6,14},{7,31},{128,136},{... | collective-permute-start | bytes 1179656 | tf_op jit(solution)/shard_map/ppermute | solution.py:43
  19.2 8.6 %collective-permute-start.3 = (f32[48,2048]{1,0:T(8,128)S(1)}, f32[48,2048]{1,0:T(8,128)S(1)}, u32[]{:S(2)}, u32[]{:S(2)}) collective-permute-start(f32[48,2048]{1,0:T(8,128)S(1)} %get-tuple-element.69), channel_id=1, source_target_pairs={{0,2},{1,135},{2,4},{3,1},{4,6},{5,3},{6,128},{7,5},{128,130},{129... | collective-permute-start | bytes 1179656 | tf_op jit(solution)/shard_map/ppermute | solution.py:43
  21.7 3.4 %copy-start = (f32[256,8192]{1,0:T(8,128)S(1)}, f32[256,8192]{1,0:T(8,128)}, u32[]{:S(2)}) copy-start(f32[256,8192]{1,0:T(8,128)} %refs_0_.1) | copy-start | bytes 25165828
  25.5 8.4 %collective-permute-start.16 = (f32[64,2048]{1,0:T(8,128)S(1)}, f32[64,2048]{1,0:T(8,128)S(1)}, u32[]{:S(2)}, u32[]{:S(2)}) collective-permute-start(f32[64,2048]{1,0:T(8,128)S(1)} %get-tuple-element.84), channel_id=1, source_target_pairs={{0,8},{1,25},{2,10},{3,27},{4,12},{5,29},{6,14},{7,31},{128,136},{... | collective-permute-start | bytes 1572872 | tf_op jit(solution)/shard_map/ppermute | solution.py:43
  25.8 8.3 %collective-permute-start.17 = (f32[64,2048]{1,0:T(8,128)S(1)}, f32[64,2048]{1,0:T(8,128)S(1)}, u32[]{:S(2)}, u32[]{:S(2)}) collective-permute-start(f32[64,2048]{1,0:T(8,128)S(1)} %get-tuple-element.85), channel_id=1, source_target_pairs={{0,2},{1,135},{2,4},{3,1},{4,6},{5,3},{6,128},{7,5},{128,130},{129... | collective-permute-start | bytes 1572872 | tf_op jit(solution)/shard_map/ppermute | solution.py:43
  27.8 16.5 %slice-start = ((s8[8388608]{0:T(1024)(128)(4,1)}), s8[4194304]{0:T(1024)(128)(4,1)S(1)}, s32[]{:S(2)}) async-start(s8[8388608]{0:T(1024)(128)(4,1)} %bitcast.3), calls=%async_computation | async-start | bytes 8388608
  27.9 11.6 %collective-permute-start.4 = (f32[64,2048]{1,0:T(8,128)S(1)}, f32[64,2048]{1,0:T(8,128)S(1)}, u32[]{:S(2)}, u32[]{:S(2)}) collective-permute-start(f32[64,2048]{1,0:T(8,128)S(1)} %get-tuple-element.70), channel_id=1, source_target_pairs={{0,8},{1,25},{2,10},{3,27},{4,12},{5,29},{6,14},{7,31},{128,136},{... | collective-permute-start | bytes 1572872 | tf_op jit(solution)/shard_map/ppermute | solution.py:43
  28.3 11.4 %collective-permute-start.5 = (f32[64,2048]{1,0:T(8,128)S(1)}, f32[64,2048]{1,0:T(8,128)S(1)}, u32[]{:S(2)}, u32[]{:S(2)}) collective-permute-start(f32[64,2048]{1,0:T(8,128)S(1)} %get-tuple-element.71), channel_id=1, source_target_pairs={{0,2},{1,135},{2,4},{3,1},{4,6},{5,3},{6,128},{7,5},{128,130},{129... | collective-permute-start | bytes 1572872 | tf_op jit(solution)/shard_map/ppermute | solution.py:43
  34.2 8.6 %copy-start.4 = (s32[256]{0:T(256)S(1)}, s32[256]{0:T(256)}, u32[]{:S(2)}) copy-start(s32[256]{0:T(256)} %param.11) | copy-start | bytes 3076
  34.2 8.6 %copy-start.5 = (f32[256]{0:T(256)S(1)}, f32[256]{0:T(256)}, u32[]{:S(2)}) copy-start(f32[256]{0:T(256)} %param.10) | copy-start | bytes 3076
  34.2 10.1 %slice-start.1 = ((s8[8388608]{0:T(1024)(128)(4,1)}), s8[4194304]{0:T(1024)(128)(4,1)S(1)}, s32[]{:S(2)}) async-start(s8[8388608]{0:T(1024)(128)(4,1)} %bitcast.3), calls=%async_computation.1 | async-start | bytes 8388608
  34.2 10.4 %collective-permute-start.20 = (f32[48,2048]{1,0:T(8,128)S(1)}, f32[48,2048]{1,0:T(8,128)S(1)}, u32[]{:S(2)}, u32[]{:S(2)}) collective-permute-start(f32[48,2048]{1,0:T(8,128)S(1)} %get-tuple-element.89), channel_id=1, source_target_pairs={{0,2},{1,135},{2,4},{3,1},{4,6},{5,3},{6,128},{7,5},{128,130},{129... | collective-permute-start | bytes 1179656 | tf_op jit(solution)/shard_map/ppermute | solution.py:43
  37.4 7.3 %collective-permute-start.19 = (f32[48,2048]{1,0:T(8,128)S(1)}, f32[48,2048]{1,0:T(8,128)S(1)}, u32[]{:S(2)}, u32[]{:S(2)}) collective-permute-start(f32[48,2048]{1,0:T(8,128)S(1)} %get-tuple-element.88), channel_id=1, source_target_pairs={{0,8},{1,25},{2,10},{3,27},{4,12},{5,29},{6,14},{7,31},{128,136},{... | collective-permute-start | bytes 1179656 | tf_op jit(solution)/shard_map/ppermute | solution.py:43
  39.8 8.8 %collective-permute-start.6 = (f32[48,2048]{1,0:T(8,128)S(1)}, f32[48,2048]{1,0:T(8,128)S(1)}, u32[]{:S(2)}, u32[]{:S(2)}) collective-permute-start(f32[48,2048]{1,0:T(8,128)S(1)} %get-tuple-element.72), channel_id=1, source_target_pairs={{0,8},{1,25},{2,10},{3,27},{4,12},{5,29},{6,14},{7,31},{128,136},{... | collective-permute-start | bytes 1179656 | tf_op jit(solution)/shard_map/ppermute | solution.py:43
  41.3 7.3 %collective-permute-start.7 = (f32[48,2048]{1,0:T(8,128)S(1)}, f32[48,2048]{1,0:T(8,128)S(1)}, u32[]{:S(2)}, u32[]{:S(2)}) collective-permute-start(f32[48,2048]{1,0:T(8,128)S(1)} %get-tuple-element.73), channel_id=1, source_target_pairs={{0,2},{1,135},{2,4},{3,1},{4,6},{5,3},{6,128},{7,5},{128,130},{129... | collective-permute-start | bytes 1179656 | tf_op jit(solution)/shard_map/ppermute | solution.py:43
  44.8 9.0 %collective-permute-start.21 = (f32[32,2048]{1,0:T(8,128)S(1)}, f32[32,2048]{1,0:T(8,128)S(1)}, u32[]{:S(2)}, u32[]{:S(2)}) collective-permute-start(f32[32,2048]{1,0:T(8,128)S(1)} %get-tuple-element.96), channel_id=1, source_target_pairs={{0,8},{1,25},{2,10},{3,27},{4,12},{5,29},{6,14},{7,31},{128,136},{... | collective-permute-start | bytes 786440 | tf_op jit(solution)/shard_map/ppermute | solution.py:43
  47.5 6.3 %collective-permute-start.22 = (f32[32,2048]{1,0:T(8,128)S(1)}, f32[32,2048]{1,0:T(8,128)S(1)}, u32[]{:S(2)}, u32[]{:S(2)}) collective-permute-start(f32[32,2048]{1,0:T(8,128)S(1)} %get-tuple-element.97), channel_id=1, source_target_pairs={{0,2},{1,135},{2,4},{3,1},{4,6},{5,3},{6,128},{7,5},{128,130},{129... | collective-permute-start | bytes 786440 | tf_op jit(solution)/shard_map/ppermute | solution.py:43
  48.7 7.6 %collective-permute-start.8 = (f32[32,2048]{1,0:T(8,128)S(1)}, f32[32,2048]{1,0:T(8,128)S(1)}, u32[]{:S(2)}, u32[]{:S(2)}) collective-permute-start(f32[32,2048]{1,0:T(8,128)S(1)} %get-tuple-element.74), channel_id=1, source_target_pairs={{0,8},{1,25},{2,10},{3,27},{4,12},{5,29},{6,14},{7,31},{128,136},{... | collective-permute-start | bytes 786440 | tf_op jit(solution)/shard_map/ppermute | solution.py:43
  50.3 6.4 %collective-permute-start.9 = (f32[32,2048]{1,0:T(8,128)S(1)}, f32[32,2048]{1,0:T(8,128)S(1)}, u32[]{:S(2)}, u32[]{:S(2)}) collective-permute-start(f32[32,2048]{1,0:T(8,128)S(1)} %get-tuple-element.75), channel_id=1, source_target_pairs={{0,2},{1,135},{2,4},{3,1},{4,6},{5,3},{6,128},{7,5},{128,130},{129... | collective-permute-start | bytes 786440 | tf_op jit(solution)/shard_map/ppermute | solution.py:43
  53.9 6.6 %collective-permute-start.23 = (f32[16,2048]{1,0:T(8,128)S(1)}, f32[16,2048]{1,0:T(8,128)S(1)}, u32[]{:S(2)}, u32[]{:S(2)}) collective-permute-start(f32[16,2048]{1,0:T(8,128)S(1)} %get-tuple-element.101), channel_id=1, source_target_pairs={{0,8},{1,25},{2,10},{3,27},{4,12},{5,29},{6,14},{7,31},{128,136},{... | collective-permute-start | bytes 393224 | tf_op jit(solution)/shard_map/ppermute | solution.py:43
  54.4 6.1 %collective-permute-start.24 = (f32[16,2048]{1,0:T(8,128)S(1)}, f32[16,2048]{1,0:T(8,128)S(1)}, u32[]{:S(2)}, u32[]{:S(2)}) collective-permute-start(f32[16,2048]{1,0:T(8,128)S(1)} %get-tuple-element.102), channel_id=1, source_target_pairs={{0,2},{1,135},{2,4},{3,1},{4,6},{5,3},{6,128},{7,5},{128,130},{129... | collective-permute-start | bytes 393224 | tf_op jit(solution)/shard_map/ppermute | solution.py:43
  56.8 8.9 %collective-permute-start.10 = (f32[16,2048]{1,0:T(8,128)S(1)}, f32[16,2048]{1,0:T(8,128)S(1)}, u32[]{:S(2)}, u32[]{:S(2)}) collective-permute-start(f32[16,2048]{1,0:T(8,128)S(1)} %get-tuple-element.76), channel_id=1, source_target_pairs={{0,8},{1,25},{2,10},{3,27},{4,12},{5,29},{6,14},{7,31},{128,136},{... | collective-permute-start | bytes 393224 | tf_op jit(solution)/shard_map/ppermute | solution.py:43
  57.3 8.3 %collective-permute-start.11 = (f32[16,2048]{1,0:T(8,128)S(1)}, f32[16,2048]{1,0:T(8,128)S(1)}, u32[]{:S(2)}, u32[]{:S(2)}) collective-permute-start(f32[16,2048]{1,0:T(8,128)S(1)} %get-tuple-element.77), channel_id=1, source_target_pairs={{0,2},{1,135},{2,4},{3,1},{4,6},{5,3},{6,128},{7,5},{128,130},{129... | collective-permute-start | bytes 393224 | tf_op jit(solution)/shard_map/ppermute | solution.py:43
  65.6 58.0 %copy-start.3 = (f32[8,2,8192]{2,1,0:T(2,128)S(1)}, f32[8,2,8192]{2,1,0:T(2,128)}, u32[]{:S(2)}) copy-start(f32[8,2,8192]{2,1,0:T(2,128)} %refs_4_.1) | copy-start | bytes 1572868
  71.0 53.8 %copy-start.2 = (f32[8,2,8192]{2,1,0:T(2,128)S(1)}, f32[8,2,8192]{2,1,0:T(2,128)}, u32[]{:S(2)}) copy-start(f32[8,2,8192]{2,1,0:T(2,128)} %refs_5_.1) | copy-start | bytes 1572868
  71.0 53.8 %copy-start.6 = (f32[64]{0:T(128)S(1)}, f32[64]{0:T(128)}, u32[]{:S(2)}) copy-start(f32[64]{0:T(128)} %param.9) | copy-start | bytes 772
  71.0 6.4 %collective-permute-start.25 = (f32[2,2,2,2,8,256]{5,4,3,2,1,0:T(8,128)S(1)}, f32[2,2,2,2,8,256]{5,4,3,2,1,0:T(8,128)S(1)}, u32[]{:S(2)}, u32[]{:S(2)}) collective-permute-start(f32[2,2,2,2,8,256]{5,4,3,2,1,0:T(8,128)S(1)} %get-tuple-element.106), channel_id=1, source_target_pairs={{0,32},{1,33},{2,34},{3,35},{4,36},{5,37},{6,38},{7,39},{128,160},... | collective-permute-start | bytes 393224 | tf_op jit(solution)/shard_map/ppermute | solution.py:43
  72.3 7.3 %collective-permute-start.26 = (f32[2,2,2,2,8,256]{5,4,3,2,1,0:T(8,128)S(1)}, f32[2,2,2,2,8,256]{5,4,3,2,1,0:T(8,128)S(1)}, u32[]{:S(2)}, u32[]{:S(2)}) collective-permute-start(f32[2,2,2,2,8,256]{5,4,3,2,1,0:T(8,128)S(1)} %get-tuple-element.107), channel_id=1, source_target_pairs={{0,64},{1,65},{2,66},{3,67},{4,68},{5,69},{6,70},{7,71},{128,192},... | collective-permute-start | bytes 393224 | tf_op jit(solution)/shard_map/ppermute | solution.py:43
  74.8 4.9 %collective-permute-start.27 = (f32[2,2,2,2,8,256]{5,4,3,2,1,0:T(8,128)S(1)}, f32[2,2,2,2,8,256]{5,4,3,2,1,0:T(8,128)S(1)}, u32[]{:S(2)}, u32[]{:S(2)}) collective-permute-start(f32[2,2,2,2,8,256]{5,4,3,2,1,0:T(8,128)S(1)} %get-tuple-element.108), channel_id=1, source_target_pairs={{0,96},{1,97},{2,98},{3,99},{4,100},{5,101},{6,102},{7,103},{128,2... | collective-permute-start | bytes 393224 | tf_op jit(solution)/shard_map/ppermute | solution.py:43
  75.9 5.3 %collective-permute-start.28 = (f32[4,2,16,256]{3,2,1,0:T(8,128)S(1)}, f32[4,2,16,256]{3,2,1,0:T(8,128)S(1)}, u32[]{:S(2)}, u32[]{:S(2)}) collective-permute-start(f32[4,2,16,256]{3,2,1,0:T(8,128)S(1)} %get-tuple-element.110), channel_id=1, source_target_pairs={{0,24},{1,9},{2,26},{3,11},{4,28},{5,13},{6,30},{7,15},{128,152},{... | collective-permute-start | bytes 393224 | tf_op jit(solution)/shard_map/ppermute | solution.py:43
  77.2 5.6 %collective-permute-start.29 = (f32[4,2,16,256]{3,2,1,0:T(8,128)S(1)}, f32[4,2,16,256]{3,2,1,0:T(8,128)S(1)}, u32[]{:S(2)}, u32[]{:S(2)}) collective-permute-start(f32[4,2,16,256]{3,2,1,0:T(8,128)S(1)} %get-tuple-element.111), channel_id=1, source_target_pairs={{0,16},{1,17},{2,18},{3,19},{4,20},{5,21},{6,22},{7,23},{128,144},... | collective-permute-start | bytes 393224 | tf_op jit(solution)/shard_map/ppermute | solution.py:43
  77.4 5.8 %collective-permute-start.30 = (f32[4,2,16,256]{3,2,1,0:T(8,128)S(1)}, f32[4,2,16,256]{3,2,1,0:T(8,128)S(1)}, u32[]{:S(2)}, u32[]{:S(2)}) collective-permute-start(f32[4,2,16,256]{3,2,1,0:T(8,128)S(1)} %get-tuple-element.112), channel_id=1, source_target_pairs={{0,8},{1,25},{2,10},{3,27},{4,12},{5,29},{6,14},{7,31},{128,136},{... | collective-permute-start | bytes 393224 | tf_op jit(solution)/shard_map/ppermute | solution.py:43
  83.4 17.7 %collective-permute-start.35 = (f32[12,2,8,256]{3,2,1,0:T(8,128)S(1)}, f32[12,2,8,256]{3,2,1,0:T(8,128)S(1)}, u32[]{:S(2)}, u32[]{:S(2)}) collective-permute-start(f32[12,2,8,256]{3,2,1,0:T(8,128)S(1)} %get-tuple-element.118), channel_id=1, source_target_pairs={{0,130},{1,7},{2,132},{3,129},{4,134},{5,131},{6,0},{7,133},{128,2... | collective-permute-start | bytes 589832 | tf_op jit(solution)/shard_map/ppermute | solution.py:43
  83.5 17.6 %collective-permute-start.36 = (f32[12,2,8,256]{3,2,1,0:T(8,128)S(1)}, f32[12,2,8,256]{3,2,1,0:T(8,128)S(1)}, u32[]{:S(2)}, u32[]{:S(2)}) collective-permute-start(f32[12,2,8,256]{3,2,1,0:T(8,128)S(1)} %get-tuple-element.119), channel_id=1, source_target_pairs={{0,132},{1,5},{2,134},{3,7},{4,0},{5,129},{6,2},{7,131},{128,4},{1... | collective-permute-start | bytes 589832 | tf_op jit(solution)/shard_map/ppermute | solution.py:43
  83.7 17.4 %collective-permute-start.37 = (f32[12,2,8,256]{3,2,1,0:T(8,128)S(1)}, f32[12,2,8,256]{3,2,1,0:T(8,128)S(1)}, u32[]{:S(2)}, u32[]{:S(2)}) collective-permute-start(f32[12,2,8,256]{3,2,1,0:T(8,128)S(1)} %get-tuple-element.120), channel_id=1, source_target_pairs={{0,134},{1,3},{2,0},{3,5},{4,2},{5,7},{6,4},{7,129},{128,6},{129,1... | collective-permute-start | bytes 589832 | tf_op jit(solution)/shard_map/ppermute | solution.py:43
  85.5 4.3 %collective-permute-start.31 = (f32[4,2,8,256]{3,2,1,0:T(8,128)S(1)}, f32[4,2,8,256]{3,2,1,0:T(8,128)S(1)}, u32[]{:S(2)}, u32[]{:S(2)}) collective-permute-start(f32[4,2,8,256]{3,2,1,0:T(8,128)S(1)} %get-tuple-element.114), channel_id=1, source_target_pairs={{0,2},{1,135},{2,4},{3,1},{4,6},{5,3},{6,128},{7,5},{128,130},{129... | collective-permute-start | bytes 196616 | tf_op jit(solution)/shard_map/ppermute | solution.py:43
  87.5 5.5 %collective-permute-start.32 = (f32[4,2,8,256]{3,2,1,0:T(8,128)S(1)}, f32[4,2,8,256]{3,2,1,0:T(8,128)S(1)}, u32[]{:S(2)}, u32[]{:S(2)}) collective-permute-start(f32[4,2,8,256]{3,2,1,0:T(8,128)S(1)} %get-tuple-element.115), channel_id=1, source_target_pairs={{0,4},{1,133},{2,6},{3,135},{4,128},{5,1},{6,130},{7,3},{128,132},... | collective-permute-start | bytes 196616 | tf_op jit(solution)/shard_map/ppermute | solution.py:43
  89.9 6.2 %collective-permute-start.33 = (f32[4,2,8,256]{3,2,1,0:T(8,128)S(1)}, f32[4,2,8,256]{3,2,1,0:T(8,128)S(1)}, u32[]{:S(2)}, u32[]{:S(2)}) collective-permute-start(f32[4,2,8,256]{3,2,1,0:T(8,128)S(1)} %get-tuple-element.116), channel_id=1, source_target_pairs={{0,6},{1,131},{2,128},{3,133},{4,130},{5,135},{6,132},{7,1},{128,1... | collective-permute-start | bytes 196616 | tf_op jit(solution)/shard_map/ppermute | solution.py:43
  93.0 8.1 %collective-permute-start.34 = (f32[4,2,8,256]{3,2,1,0:T(8,128)S(1)}, f32[4,2,8,256]{3,2,1,0:T(8,128)S(1)}, u32[]{:S(2)}, u32[]{:S(2)}) collective-permute-start(f32[4,2,8,256]{3,2,1,0:T(8,128)S(1)} %get-tuple-element.117), channel_id=1, source_target_pairs={{0,128},{1,129},{2,130},{3,131},{4,132},{5,133},{6,134},{7,135},{1... | collective-permute-start | bytes 196616 | tf_op jit(solution)/shard_map/ppermute | solution.py:43
  101.5 5.4 %collective-permute-start.38 = (f32[4,2,2,8,256]{4,3,2,1,0:T(8,128)S(1)}, f32[4,2,2,8,256]{4,3,2,1,0:T(8,128)S(1)}, u32[]{:S(2)}, u32[]{:S(2)}) collective-permute-start(f32[4,2,2,8,256]{4,3,2,1,0:T(8,128)S(1)} %get-tuple-element.122), channel_id=1, source_target_pairs={{0,8},{1,9},{2,10},{3,11},{4,12},{5,13},{6,14},{7,15},{128,136},{1... | collective-permute-start | bytes 393224 | tf_op jit(solution)/shard_map/ppermute | solution.py:43
  101.6 7.7 %collective-permute-start.39 = (f32[4,2,2,8,256]{4,3,2,1,0:T(8,128)S(1)}, f32[4,2,2,8,256]{4,3,2,1,0:T(8,128)S(1)}, u32[]{:S(2)}, u32[]{:S(2)}) collective-permute-start(f32[4,2,2,8,256]{4,3,2,1,0:T(8,128)S(1)} %get-tuple-element.123), channel_id=1, source_target_pairs={{0,16},{1,17},{2,18},{3,19},{4,20},{5,21},{6,22},{7,23},{128,144},... | collective-permute-start | bytes 393224 | tf_op jit(solution)/shard_map/ppermute | solution.py:43
  105.5 4.1 %collective-permute-start.40 = (f32[4,2,2,8,256]{4,3,2,1,0:T(8,128)S(1)}, f32[4,2,2,8,256]{4,3,2,1,0:T(8,128)S(1)}, u32[]{:S(2)}, u32[]{:S(2)}) collective-permute-start(f32[4,2,2,8,256]{4,3,2,1,0:T(8,128)S(1)} %get-tuple-element.124), channel_id=1, source_target_pairs={{0,24},{1,25},{2,26},{3,27},{4,28},{5,29},{6,30},{7,31},{128,152},... | collective-permute-start | bytes 393224 | tf_op jit(solution)/shard_map/ppermute | solution.py:43
  109.7 15.2 %collective-permute-start.41 = (f32[4,4,2,8,256]{4,3,2,1,0:T(8,128)S(1)}, f32[4,4,2,8,256]{4,3,2,1,0:T(8,128)S(1)}, u32[]{:S(2)}, u32[]{:S(2)}) collective-permute-start(f32[4,4,2,8,256]{4,3,2,1,0:T(8,128)S(1)} %swap_pack.1), channel_id=1, source_target_pairs={{0,1},{1,0},{2,3},{3,2},{4,5},{5,4},{6,7},{7,6},{128,129},{129,128... | collective-permute-start | bytes 786440 | tf_op jit(solution)/shard_map/ppermute | solution.py:43
where the time goes:
time: 128 us
  starting transfers between devices  80 us (62%)
  waiting for transfers between devices  24.5 us (19%)
  Pallas kernels  17.9 us (14%)
  local copies, waits for them, and re-layouts  4.47 us (3%)
    ppermute x42, starting transfers between devices, shift(): return lax.ppermute(array, BOTH, moved(**steps))  80 us
    ppermute x42, waiting for transfers between devices, shift(): return lax.ppermute(array, BOTH, moved(**steps))  24.5 us
    pallas_call x19, Pallas kernels, call(): pl.pallas_call(kernel, in_specs=[VMEM] * len(operands), out_specs=[VMEM]...  16.6 us
    unnamed x18, local copies, waits for them, and re-layouts  4.47 us
  transfers between devices with their start and end apart: 42, of which 18 were waited for; matrix products, arithmetic and copies ran while one was open for 0% of the time, Pallas kernels for 7%

commit v1 on v0

--- a/solution.py
+++ b/solution.py
@@ -12,7 +12,7 @@
 HALF = NP // 2
 STREAMS = 2
 RANGE = NP // (2 * STREAMS)
-TILE = 512
+TILE = 1024
 ROWS = 256
 COLS = 256
 BOTH = ("ia", "ja")
@@ -48,12 +48,12 @@
     return high, (value - high.astype(F32)).astype(BF16)
 
 
-def multiply(pieces, own, partner, start, total):
+def multiply(pieces, own, partner, start, total, width):
     dims = (((1,), (1,)), ((), ()))
 
     def tile(k, carry):
         def columns(first):
-            return pl.ds(pl.multiple_of(k * TILE + first, TILE), TILE)
+            return pl.ds(pl.multiple_of(k * width + first, width), width)
 
         parts = [ref[row : row + rows, columns(first)] for ref, row, rows, first in pieces]
         t_high, t_low = split(jnp.concatenate(parts, axis=0))
@@ -65,7 +65,7 @@
         total[...] += part
         return carry
 
-    lax.fori_loop(0, RANGE // TILE, tile, 0)
+    lax.fori_loop(0, RANGE // width, tile, 0)
 
 
 def prepare_kernel(order, energy, pair, turn):
@@ -172,7 +172,8 @@
 def product(stream, refs, own, partner, total, use):
     for half, (pieces, slots) in enumerate(stream_pieces(stream, refs)):
         total[...] = jnp.zeros_like(total)
-        multiply(pieces, own, partner, (stream * 2 + half) * RANGE % HALF, total)
+        width = TILE if stream == STREAMS - 1 else TILE // 2
+        multiply(pieces, own, partner, (stream * 2 + half) * RANGE % HALF, total, width)
         for block, slot in enumerate(slots):
             for v in range(2):
                 use(half, v, slot, total[block * 16 : block * 16 + 16, v * COLS : (v + 1) * COLS])
@@ -320,15 +321,19 @@
     first = jnp.sum(jnp.where(lane == i, occupied[...], 0.0), axis=1, keepdims=True)
     second = jnp.sum(jnp.where(lane == j, occupied[...], 0.0), axis=1, keepdims=True)
     order = (0, 2, 1, 3)
-    for e in range(4):
-        for z_low in range(4):
-            for core in range(2):
-                kept, given = mirror[e][z_low, c, core], swapped[e, z_low, core]
-                a, b = jnp.where(c == 0, kept, given), jnp.where(c == 0, given, kept)
-                rows = [s[m * 4 + n : m * 4 + n + 1] for m in range(2) for s in (a, b) for n in order]
-                column = (z_low % 2 * 2 + core) * COLS
-                group = e * 2 + z_low // 2
-                moved_ref[group * 16 : group * 16 + 16, column : column + COLS] = jnp.concatenate(rows, axis=0)
+
+    def gather(n, carry):
+        z_low, core = n // 2, lax.rem(n, 2)
+        column = pl.ds(pl.multiple_of((lax.rem(z_low, 2) * 2 + core) * COLS, COLS), COLS)
+        for e in range(4):
+            kept, given = mirror[e][z_low, c, core], swapped[e, z_low, core]
+            a, b = jnp.where(c == 0, kept, given), jnp.where(c == 0, given, kept)
+            rows = [half[m * 4 + r : m * 4 + r + 1] for m in range(2) for half in (a, b) for r in order]
+            at_rows = pl.ds(pl.multiple_of((e * 2 + z_low // 2) * 16, 16), 16)
+            moved_ref[at_rows, column] = jnp.concatenate(rows, axis=0)
+        return carry
+
+    lax.fori_loop(0, 8, gather, 0)
     value = moved_ref[...]
 
     def columns(n, carry):

time: 128 us -> 127 us (level)
  no operation moved by 1% of the time
where the time goes in v1:
time: 127 us
  starting transfers between devices  80 us (63%)
  waiting for transfers between devices  24.5 us (19%)
  Pallas kernels  17.3 us (14%)
  local copies, waits for them, and re-layouts  4.47 us (4%)
    ppermute x42, starting transfers between devices, shift(): return lax.ppermute(array, BOTH, moved(**steps))  80 us
    ppermute x42, waiting for transfers between devices, shift(): return lax.ppermute(array, BOTH, moved(**steps))  24.5 us
    pallas_call x19, Pallas kernels, call(): pl.pallas_call(kernel, in_specs=[VMEM] * len(operands), out_specs=[VMEM]...  16 us
    unnamed x18, local copies, waits for them, and re-layouts  4.47 us
  transfers between devices with their start and end apart: 42, of which 18 were waited for; matrix products, arithmetic and copies ran while one was open for 0% of the time, Pallas kernels for 7%

profile of v1, /device:TPU:1, one launch (start us, length us, event | category | flops | bytes accessed | tf_op | source)
XLA Modules:
  0.0 127.3 jit_solution(13946650016896828706)
XLA Ops:
  0.6 3.3 %collective-permute-start.18 = (f32[256,8192]{1,0:T(8,128)}, f32[256,8192]{1,0:T(8,128)S(1)}, u32[]{:S(2)}, u32[]{:S(2)}) collective-permute-start(f32[256,8192]{1,0:T(8,128)} %refs_0_.1), channel_id=1, source_target_pairs={{0,1},{1,0},{2,3},{3,2},{4,5},{5,4},{6,7},{7,6},{128,129},{129,128... | collective-permute-start | bytes 25165832 | tf_op jit(solution)/shard_map/ppermute | solution.py:43
  4.0 1.0 copy-done.1
  5.0 0.2 relayout.1
  5.2 1.1 collective-permute-start.12
  6.3 5.6 %collective-permute-start.13 = (f32[32,2048]{1,0:T(8,128)S(1)}, f32[32,2048]{1,0:T(8,128)S(1)}, u32[]{:S(2)}, u32[]{:S(2)}) collective-permute-start(f32[32,2048]{1,0:T(8,128)S(1)} %get-tuple-element.79), channel_id=1, source_target_pairs={{0,2},{1,135},{2,4},{3,1},{4,6},{5,3},{6,128},{7,5},{128,130},{129... | collective-permute-start | bytes 786440 | tf_op jit(solution)/shard_map/ppermute | solution.py:43
  11.9 0.5 collective-permute-start
  12.3 0.7 collective-permute-start.1
  13.1 2.1 %collective-permute-done.13.refs_1_.refs_2_ = f32[32,2048]{1,0:T(8,128)S(1)} collective-permute-done((f32[32,2048]{1,0:T(8,128)S(1)}, f32[32,2048]{1,0:T(8,128)S(1)}, u32[]{:S(2)}, u32[]{:S(2)}) %collective-permute-start.13) | collective-permute-done | bytes 262176 | tf_op jit(solution)/shard_map/ppermute | solution.py:43
  15.2 0.5 collective-permute-start.14
  15.8 3.1 %collective-permute-start.15 = (f32[48,2048]{1,0:T(8,128)S(1)}, f32[48,2048]{1,0:T(8,128)S(1)}, u32[]{:S(2)}, u32[]{:S(2)}) collective-permute-start(f32[48,2048]{1,0:T(8,128)S(1)} %get-tuple-element.81), channel_id=1, source_target_pairs={{0,2},{1,135},{2,4},{3,1},{4,6},{5,3},{6,128},{7,5},{128,130},{129... | collective-permute-start | bytes 1179656 | tf_op jit(solution)/shard_map/ppermute | solution.py:43
  19.0 0.2 collective-permute-start.2
  19.2 2.5 %collective-permute-start.3 = (f32[48,2048]{1,0:T(8,128)S(1)}, f32[48,2048]{1,0:T(8,128)S(1)}, u32[]{:S(2)}, u32[]{:S(2)}) collective-permute-start(f32[48,2048]{1,0:T(8,128)S(1)} %get-tuple-element.69), channel_id=1, source_target_pairs={{0,2},{1,135},{2,4},{3,1},{4,6},{5,3},{6,128},{7,5},{128,130},{129... | collective-permute-start | bytes 1179656 | tf_op jit(solution)/shard_map/ppermute | solution.py:43
  21.7 3.4 %copy-done = f32[256,8192]{1,0:T(8,128)S(1)} copy-done((f32[256,8192]{1,0:T(8,128)S(1)}, f32[256,8192]{1,0:T(8,128)}, u32[]{:S(2)}) %copy-start) | copy-done | bytes 8388632
  25.1 0.3 load.4.refs_13_
  25.5 0.2 collective-permute-start.16
  25.8 1.5 %collective-permute-start.17 = (f32[64,2048]{1,0:T(8,128)S(1)}, f32[64,2048]{1,0:T(8,128)S(1)}, u32[]{:S(2)}, u32[]{:S(2)}) collective-permute-start(f32[64,2048]{1,0:T(8,128)S(1)} %get-tuple-element.85), channel_id=1, source_target_pairs={{0,2},{1,135},{2,4},{3,1},{4,6},{5,3},{6,128},{7,5},{128,130},{129... | collective-permute-start | bytes 1572872 | tf_op jit(solution)/shard_map/ppermute | solution.py:43
  27.3 0.5 collective-permute-done.3.refs_1_.refs_4_
  27.9 0.4 collective-permute-start.4
  28.3 3.2 %collective-permute-start.5 = (f32[64,2048]{1,0:T(8,128)S(1)}, f32[64,2048]{1,0:T(8,128)S(1)}, u32[]{:S(2)}, u32[]{:S(2)}) collective-permute-start(f32[64,2048]{1,0:T(8,128)S(1)} %get-tuple-element.71), channel_id=1, source_target_pairs={{0,2},{1,135},{2,4},{3,1},{4,6},{5,3},{6,128},{7,5},{128,130},{129... | collective-permute-start | bytes 1572872 | tf_op jit(solution)/shard_map/ppermute | solution.py:43
  31.5 2.4 %collective-permute-done.16.refs_0_.refs_5_ = f32[64,2048]{1,0:T(8,128)S(1)} collective-permute-done((f32[64,2048]{1,0:T(8,128)S(1)}, f32[64,2048]{1,0:T(8,128)S(1)}, u32[]{:S(2)}, u32[]{:S(2)}) %collective-permute-start.16) | collective-permute-done | bytes 524320 | tf_op jit(solution)/shard_map/ppermute | solution.py:43
  34.2 2.8 %collective-permute-start.20 = (f32[48,2048]{1,0:T(8,128)S(1)}, f32[48,2048]{1,0:T(8,128)S(1)}, u32[]{:S(2)}, u32[]{:S(2)}) collective-permute-start(f32[48,2048]{1,0:T(8,128)S(1)} %get-tuple-element.89), channel_id=1, source_target_pairs={{0,2},{1,135},{2,4},{3,1},{4,6},{5,3},{6,128},{7,5},{128,130},{129... | collective-permute-start | bytes 1179656 | tf_op jit(solution)/shard_map/ppermute | solution.py:43
  37.1 0.3 load.5.refs_14_
  37.5 2.1 %collective-permute-done.4.refs_0_.refs_5_ = f32[64,2048]{1,0:T(8,128)S(1)} collective-permute-done((f32[64,2048]{1,0:T(8,128)S(1)}, f32[64,2048]{1,0:T(8,128)S(1)}, u32[]{:S(2)}, u32[]{:S(2)}) %collective-permute-start.4) | collective-permute-done | bytes 524320 | tf_op jit(solution)/shard_map/ppermute | solution.py:43
  39.8 1.5 %collective-permute-start.6 = (f32[48,2048]{1,0:T(8,128)S(1)}, f32[48,2048]{1,0:T(8,128)S(1)}, u32[]{:S(2)}, u32[]{:S(2)}) collective-permute-start(f32[48,2048]{1,0:T(8,128)S(1)} %get-tuple-element.72), channel_id=1, source_target_pairs={{0,8},{1,25},{2,10},{3,27},{4,12},{5,29},{6,14},{7,31},{128,136},{... | collective-permute-start | bytes 1179656 | tf_op jit(solution)/shard_map/ppermute | solution.py:43
  41.3 1.5 %collective-permute-start.7 = (f32[48,2048]{1,0:T(8,128)S(1)}, f32[48,2048]{1,0:T(8,128)S(1)}, u32[]{:S(2)}, u32[]{:S(2)}) collective-permute-start(f32[48,2048]{1,0:T(8,128)S(1)} %get-tuple-element.73), channel_id=1, source_target_pairs={{0,2},{1,135},{2,4},{3,1},{4,6},{5,3},{6,128},{7,5},{128,130},{129... | collective-permute-start | bytes 1179656 | tf_op jit(solution)/shard_map/ppermute | solution.py:43
  42.8 1.5 %prepare.1 = (f32[8,1024]{1,0:T(8,128)S(1)}, bf16[1024,1024]{1,0:T(8,128)(2,1)S(1)}) custom-call(s32[1,256]{1,0:T(1,128)S(1)} %bitcast.5, f32[1,256]{1,0:T(1,128)S(1)} %bitcast.6), custom_call_target="tpu_custom_call" | custom-call | tf_op jit(solution)/shard_map/prepare/pallas_call | solution.py:364
  44.3 0.3 load.6.refs_13_
  44.8 2.8 %collective-permute-start.21 = (f32[32,2048]{1,0:T(8,128)S(1)}, f32[32,2048]{1,0:T(8,128)S(1)}, u32[]{:S(2)}, u32[]{:S(2)}) collective-permute-start(f32[32,2048]{1,0:T(8,128)S(1)} %get-tuple-element.96), channel_id=1, source_target_pairs={{0,8},{1,25},{2,10},{3,27},{4,12},{5,29},{6,14},{7,31},{128,136},{... | collective-permute-start | bytes 786440 | tf_op jit(solution)/shard_map/ppermute | solution.py:43
  47.5 1.1 collective-permute-done.6.refs_0_.refs_7_
  48.7 1.7 %collective-permute-start.8 = (f32[32,2048]{1,0:T(8,128)S(1)}, f32[32,2048]{1,0:T(8,128)S(1)}, u32[]{:S(2)}, u32[]{:S(2)}) collective-permute-start(f32[32,2048]{1,0:T(8,128)S(1)} %get-tuple-element.74), channel_id=1, source_target_pairs={{0,8},{1,25},{2,10},{3,27},{4,12},{5,29},{6,14},{7,31},{128,136},{... | collective-permute-start | bytes 786440 | tf_op jit(solution)/shard_map/ppermute | solution.py:43
  50.3 3.1 %collective-permute-start.9 = (f32[32,2048]{1,0:T(8,128)S(1)}, f32[32,2048]{1,0:T(8,128)S(1)}, u32[]{:S(2)}, u32[]{:S(2)}) collective-permute-start(f32[32,2048]{1,0:T(8,128)S(1)} %get-tuple-element.75), channel_id=1, source_target_pairs={{0,2},{1,135},{2,4},{3,1},{4,6},{5,3},{6,128},{7,5},{128,130},{129... | collective-permute-start | bytes 786440 | tf_op jit(solution)/shard_map/ppermute | solution.py:43
  53.4 0.3 load.7.refs_14_
  53.9 0.5 collective-permute-start.23
  54.4 1.8 %collective-permute-start.24 = (f32[16,2048]{1,0:T(8,128)S(1)}, f32[16,2048]{1,0:T(8,128)S(1)}, u32[]{:S(2)}, u32[]{:S(2)}) collective-permute-start(f32[16,2048]{1,0:T(8,128)S(1)} %get-tuple-element.102), channel_id=1, source_target_pairs={{0,2},{1,135},{2,4},{3,1},{4,6},{5,3},{6,128},{7,5},{128,130},{129... | collective-permute-start | bytes 393224 | tf_op jit(solution)/shard_map/ppermute | solution.py:43
  56.2 0.5 collective-permute-done.9.refs_1_.refs_10_
  56.8 0.5 collective-permute-start.10
  57.3 3.1 %collective-permute-start.11 = (f32[16,2048]{1,0:T(8,128)S(1)}, f32[16,2048]{1,0:T(8,128)S(1)}, u32[]{:S(2)}, u32[]{:S(2)}) collective-permute-start(f32[16,2048]{1,0:T(8,128)S(1)} %get-tuple-element.77), channel_id=1, source_target_pairs={{0,2},{1,135},{2,4},{3,1},{4,6},{5,3},{6,128},{7,5},{128,130},{129... | collective-permute-start | bytes 393224 | tf_op jit(solution)/shard_map/ppermute | solution.py:43
  60.5 5.2 %stream.1.refs_15_ = f32[2,16,16,256]{3,2,1,0:T(8,128)S(1)} custom-call(f32[16,8192]{1,0:T(8,128)S(1)} %get-tuple-element.65.refs_0_, f32[32,2048]{1,0:T(8,128)S(1)} %collective-permute-done.12.refs_0_.refs_1_, f32[32,2048]{1,0:T(8,128)S(1)} %collective-permute-done.13.refs_1_.refs_2_, f32[48,2048]{1,0:T(8,128)S(1)} %collective-permute-done.14.refs_0_.refs_3_, ...), custom_call_target="tpu_custom_call" | custom-call | flops 3221225472 | bytes 6291456 | tf_op jit(solution)/shard_map/stream/pallas_call | solution.py:364
  65.7 4.5 %last_stream.1 = (f32[4,2,16,256]{3,2,1,0:T(8,128)S(1)}, f32[4,2,16,256]{3,2,1,0:T(8,128)S(1)}, f32[4,2,16,256]{3,2,1,0:T(8,128)S(1)}, f32[4,2,16,256]{3,2,1,0:T...) custom-call(f32[16,8192]{1,0:T(8,128)S(1)} %get-tuple-element.65.ref, ...), custom_call_target="tpu_custom_call" | custom-call | flops 3221225472 | bytes 6291456 | tf_op jit(solution)/shard_map/last_stream/pallas_call | solution.py:364
  70.3 1.3 %collective-permute-start.25 = (f32[2,2,2,2,8,256]{5,4,3,2,1,0:T(8,128)S(1)}, f32[2,2,2,2,8,256]{5,4,3,2,1,0:T(8,128)S(1)}, u32[]{:S(2)}, u32[]{:S(2)}) collective-permute-start(f32[2,2,2,2,8,256]{5,4,3,2,1,0:T(8,128)S(1)} %get-tuple-element.106), channel_id=1, source_target_pairs={{0,32},{1,33},{2,34},{3,35},{4,36},{5,37},{6,38},{7,39},{128,160},... | collective-permute-start | bytes 393224 | tf_op jit(solution)/shard_map/ppermute | solution.py:43
  71.5 2.5 %collective-permute-start.26 = (f32[2,2,2,2,8,256]{5,4,3,2,1,0:T(8,128)S(1)}, f32[2,2,2,2,8,256]{5,4,3,2,1,0:T(8,128)S(1)}, u32[]{:S(2)}, u32[]{:S(2)}) collective-permute-start(f32[2,2,2,2,8,256]{5,4,3,2,1,0:T(8,128)S(1)} %get-tuple-element.107), channel_id=1, source_target_pairs={{0,64},{1,65},{2,66},{3,67},{4,68},{5,69},{6,70},{7,71},{128,192},... | collective-permute-start | bytes 393224 | tf_op jit(solution)/shard_map/ppermute | solution.py:43
  74.0 1.1 collective-permute-start.27
  75.1 1.3 %collective-permute-start.28 = (f32[4,2,16,256]{3,2,1,0:T(8,128)S(1)}, f32[4,2,16,256]{3,2,1,0:T(8,128)S(1)}, u32[]{:S(2)}, u32[]{:S(2)}) collective-permute-start(f32[4,2,16,256]{3,2,1,0:T(8,128)S(1)} %get-tuple-element.110), channel_id=1, source_target_pairs={{0,24},{1,9},{2,26},{3,11},{4,28},{5,13},{6,30},{7,15},{128,152},{... | collective-permute-start | bytes 393224 | tf_op jit(solution)/shard_map/ppermute | solution.py:43
  76.6 2.2 %collective-permute-start.30 = (f32[4,2,16,256]{3,2,1,0:T(8,128)S(1)}, f32[4,2,16,256]{3,2,1,0:T(8,128)S(1)}, u32[]{:S(2)}, u32[]{:S(2)}) collective-permute-start(f32[4,2,16,256]{3,2,1,0:T(8,128)S(1)} %get-tuple-element.112), channel_id=1, source_target_pairs={{0,8},{1,25},{2,10},{3,27},{4,12},{5,29},{6,14},{7,31},{128,136},{... | collective-permute-start | bytes 393224 | tf_op jit(solution)/shard_map/ppermute | solution.py:43
  78.9 1.6 %collective-permute-done.28.refs_5_ = f32[4,2,16,256]{3,2,1,0:T(8,128)S(1)} collective-permute-done((f32[4,2,16,256]{3,2,1,0:T(8,128)S(1)}, f32[4,2,16,256]{3,2,1,0:T(8,128)S(1)}, u32[]{:S(2)}, u32[]{:S(2)}) %collective-permute-start.28) | collective-permute-done | bytes 131104 | tf_op jit(solution)/shard_map/ppermute | solution.py:43
  80.5 1.6 %collective-permute-done.29.refs_6_ = f32[4,2,16,256]{3,2,1,0:T(8,128)S(1)} collective-permute-done((f32[4,2,16,256]{3,2,1,0:T(8,128)S(1)}, f32[4,2,16,256]{3,2,1,0:T(8,128)S(1)}, u32[]{:S(2)}, u32[]{:S(2)}) %collective-permute-start.29) | collective-permute-done | bytes 131104 | tf_op jit(solution)/shard_map/ppermute | solution.py:43
  82.1 0.4 collective-permute-done.30.refs_7_
  82.9 1.9 %collective-permute-start.37 = (f32[12,2,8,256]{3,2,1,0:T(8,128)S(1)}, f32[12,2,8,256]{3,2,1,0:T(8,128)S(1)}, u32[]{:S(2)}, u32[]{:S(2)}) collective-permute-start(f32[12,2,8,256]{3,2,1,0:T(8,128)S(1)} %get-tuple-element.120), channel_id=1, source_target_pairs={{0,134},{1,3},{2,0},{3,5},{4,2},{5,7},{6,4},{7,129},{128,6},{129,1... | collective-permute-start | bytes 589832 | tf_op jit(solution)/shard_map/ppermute | solution.py:43
  84.8 1.9 %collective-permute-start.31 = (f32[4,2,8,256]{3,2,1,0:T(8,128)S(1)}, f32[4,2,8,256]{3,2,1,0:T(8,128)S(1)}, u32[]{:S(2)}, u32[]{:S(2)}) collective-permute-start(f32[4,2,8,256]{3,2,1,0:T(8,128)S(1)} %get-tuple-element.114), channel_id=1, source_target_pairs={{0,2},{1,135},{2,4},{3,1},{4,6},{5,3},{6,128},{7,5},{128,130},{129... | collective-permute-start | bytes 196616 | tf_op jit(solution)/shard_map/ppermute | solution.py:43
  86.7 1.2 collective-permute-start.32
  87.9 1.2 collective-permute-done.31.refs_1_
  89.1 3.2 %collective-permute-start.33 = (f32[4,2,8,256]{3,2,1,0:T(8,128)S(1)}, f32[4,2,8,256]{3,2,1,0:T(8,128)S(1)}, u32[]{:S(2)}, u32[]{:S(2)}) collective-permute-start(f32[4,2,8,256]{3,2,1,0:T(8,128)S(1)} %get-tuple-element.116), channel_id=1, source_target_pairs={{0,6},{1,131},{2,128},{3,133},{4,130},{5,135},{6,132},{7,1},{128,1... | collective-permute-start | bytes 196616 | tf_op jit(solution)/shard_map/ppermute | solution.py:43
  92.3 2.6 %collective-permute-start.34 = (f32[4,2,8,256]{3,2,1,0:T(8,128)S(1)}, f32[4,2,8,256]{3,2,1,0:T(8,128)S(1)}, u32[]{:S(2)}, u32[]{:S(2)}) collective-permute-start(f32[4,2,8,256]{3,2,1,0:T(8,128)S(1)} %get-tuple-element.117), channel_id=1, source_target_pairs={{0,128},{1,129},{2,130},{3,131},{4,132},{5,133},{6,134},{7,135},{1... | collective-permute-start | bytes 196616 | tf_op jit(solution)/shard_map/ppermute | solution.py:43
  94.9 0.4 collective-permute-done.33.refs_3_
  95.3 5.0 %collective-permute-done.34.refs_4_ = f32[4,2,8,256]{3,2,1,0:T(8,128)S(1)} collective-permute-done((f32[4,2,8,256]{3,2,1,0:T(8,128)S(1)}, f32[4,2,8,256]{3,2,1,0:T(8,128)S(1)}, u32[]{:S(2)}, u32[]{:S(2)}) %collective-permute-start.34) | collective-permute-done | bytes 65568 | tf_op jit(solution)/shard_map/ppermute | solution.py:43
  100.3 0.3 y_pack.1
  100.8 3.9 %collective-permute-start.39 = (f32[4,2,2,8,256]{4,3,2,1,0:T(8,128)S(1)}, f32[4,2,2,8,256]{4,3,2,1,0:T(8,128)S(1)}, u32[]{:S(2)}, u32[]{:S(2)}) collective-permute-start(f32[4,2,2,8,256]{4,3,2,1,0:T(8,128)S(1)} %get-tuple-element.123), channel_id=1, source_target_pairs={{0,16},{1,17},{2,18},{3,19},{4,20},{5,21},{6,22},{7,23},{128,144},... | collective-permute-start | bytes 393224 | tf_op jit(solution)/shard_map/ppermute | solution.py:43
  104.8 1.3 %collective-permute-done.38.refs_1_ = f32[4,2,2,8,256]{4,3,2,1,0:T(8,128)S(1)} collective-permute-done((f32[4,2,2,8,256]{4,3,2,1,0:T(8,128)S(1)}, f32[4,2,2,8,256]{4,3,2,1,0:T(8,128)S(1)}, u32[]{:S(2)}, u32[]{:S(2)}) %collective-permute-start.38) | collective-permute-done | bytes 131104 | tf_op jit(solution)/shard_map/ppermute | solution.py:43
  106.1 2.4 %collective-permute-done.39.refs_2_ = f32[4,2,2,8,256]{4,3,2,1,0:T(8,128)S(1)} collective-permute-done((f32[4,2,2,8,256]{4,3,2,1,0:T(8,128)S(1)}, f32[4,2,2,8,256]{4,3,2,1,0:T(8,128)S(1)}, u32[]{:S(2)}, u32[]{:S(2)}) %collective-permute-start.39) | collective-permute-done | bytes 131104 | tf_op jit(solution)/shard_map/ppermute | solution.py:43
  108.5 0.4 collective-permute-done.40.refs_3_
  108.9 14.0 %collective-permute-start.41 = (f32[4,4,2,8,256]{4,3,2,1,0:T(8,128)S(1)}, f32[4,4,2,8,256]{4,3,2,1,0:T(8,128)S(1)}, u32[]{:S(2)}, u32[]{:S(2)}) collective-permute-start(f32[4,4,2,8,256]{4,3,2,1,0:T(8,128)S(1)} %swap_pack.1), channel_id=1, source_target_pairs={{0,1},{1,0},{2,3},{3,2},{4,5},{5,4},{6,7},{7,6},{128,129},{129,128... | collective-permute-start | bytes 786440 | tf_op jit(solution)/shard_map/ppermute | solution.py:43
  122.9 0.2 base.1.refs_6_
  123.1 0.9 collective-permute-done.41.refs_4_
  124.1 3.2 %final.1 = (f32[8,2,8192]{2,1,0:T(2,128)}, f32[8,2,8192]{2,1,0:T(2,128)}) custom-call(f32[4,2,2,8,256]{4,3,2,1,0:T(8,128)S(1)} %get-tuple-element.121.refs_0_, f32[4,2,2,8,256]{4,3,2,1,0:T(8,128)S(1)} %collective-permute-done.38.refs_1_, f32[4,2,2,8,256]{4,3,2,1,0:T(8,128)S(1)} %collective-permute-done.39.refs_2_, ...), custom_call_target="tpu_custom_call" | custom-call | tf_op jit(solution)/shard_map/final/pallas_call | solution.py:364
  (62 shorter events, 2.0 us)
Async XLA Ops:
  0.6 36.4 %collective-permute-start.18 = (f32[256,8192]{1,0:T(8,128)}, f32[256,8192]{1,0:T(8,128)S(1)}, u32[]{:S(2)}, u32[]{:S(2)}) collective-permute-start(f32[256,8192]{1,0:T(8,128)} %refs_0_.1), channel_id=1, source_target_pairs={{0,1},{1,0},{2,3},{3,2},{4,5},{5,4},{6,7},{7,6},{128,129},{129,128... | collective-permute-start | bytes 25165832 | tf_op jit(solution)/shard_map/ppermute | solution.py:43
  4.0 1.0 copy-start.1
  5.2 7.8 %collective-permute-start.12 = (f32[32,2048]{1,0:T(8,128)S(1)}, f32[32,2048]{1,0:T(8,128)S(1)}, u32[]{:S(2)}, u32[]{:S(2)}) collective-permute-start(f32[32,2048]{1,0:T(8,128)S(1)} %get-tuple-element.78), channel_id=1, source_target_pairs={{0,8},{1,25},{2,10},{3,27},{4,12},{5,29},{6,14},{7,31},{128,136},{... | collective-permute-start | bytes 786440 | tf_op jit(solution)/shard_map/ppermute | solution.py:43
  6.3 8.9 %collective-permute-start.13 = (f32[32,2048]{1,0:T(8,128)S(1)}, f32[32,2048]{1,0:T(8,128)S(1)}, u32[]{:S(2)}, u32[]{:S(2)}) collective-permute-start(f32[32,2048]{1,0:T(8,128)S(1)} %get-tuple-element.79), channel_id=1, source_target_pairs={{0,2},{1,135},{2,4},{3,1},{4,6},{5,3},{6,128},{7,5},{128,130},{129... | collective-permute-start | bytes 786440 | tf_op jit(solution)/shard_map/ppermute | solution.py:43
  11.9 7.0 %collective-permute-start = (f32[32,2048]{1,0:T(8,128)S(1)}, f32[32,2048]{1,0:T(8,128)S(1)}, u32[]{:S(2)}, u32[]{:S(2)}) collective-permute-start(f32[32,2048]{1,0:T(8,128)S(1)} %get-tuple-element.66), channel_id=1, source_target_pairs={{0,8},{1,25},{2,10},{3,27},{4,12},{5,29},{6,14},{7,31},{128,136},{... | collective-permute-start | bytes 786440 | tf_op jit(solution)/shard_map/ppermute | solution.py:43
  12.3 6.6 %collective-permute-start.1 = (f32[32,2048]{1,0:T(8,128)S(1)}, f32[32,2048]{1,0:T(8,128)S(1)}, u32[]{:S(2)}, u32[]{:S(2)}) collective-permute-start(f32[32,2048]{1,0:T(8,128)S(1)} %get-tuple-element.67), channel_id=1, source_target_pairs={{0,2},{1,135},{2,4},{3,1},{4,6},{5,3},{6,128},{7,5},{128,130},{129... | collective-permute-start | bytes 786440 | tf_op jit(solution)/shard_map/ppermute | solution.py:43
  15.2 10.2 %collective-permute-start.14 = (f32[48,2048]{1,0:T(8,128)S(1)}, f32[48,2048]{1,0:T(8,128)S(1)}, u32[]{:S(2)}, u32[]{:S(2)}) collective-permute-start(f32[48,2048]{1,0:T(8,128)S(1)} %get-tuple-element.80), channel_id=1, source_target_pairs={{0,8},{1,25},{2,10},{3,27},{4,12},{5,29},{6,14},{7,31},{128,136},{... | collective-permute-start | bytes 1179656 | tf_op jit(solution)/shard_map/ppermute | solution.py:43
  15.8 9.7 %collective-permute-start.15 = (f32[48,2048]{1,0:T(8,128)S(1)}, f32[48,2048]{1,0:T(8,128)S(1)}, u32[]{:S(2)}, u32[]{:S(2)}) collective-permute-start(f32[48,2048]{1,0:T(8,128)S(1)} %get-tuple-element.81), channel_id=1, source_target_pairs={{0,2},{1,135},{2,4},{3,1},{4,6},{5,3},{6,128},{7,5},{128,130},{129... | collective-permute-start | bytes 1179656 | tf_op jit(solution)/shard_map/ppermute | solution.py:43
  19.0 8.3 %collective-permute-start.2 = (f32[48,2048]{1,0:T(8,128)S(1)}, f32[48,2048]{1,0:T(8,128)S(1)}, u32[]{:S(2)}, u32[]{:S(2)}) collective-permute-start(f32[48,2048]{1,0:T(8,128)S(1)} %get-tuple-element.68), channel_id=1, source_target_pairs={{0,8},{1,25},{2,10},{3,27},{4,12},{5,29},{6,14},{7,31},{128,136},{... | collective-permute-start | bytes 1179656 | tf_op jit(solution)/shard_map/ppermute | solution.py:43
  19.2 8.6 %collective-permute-start.3 = (f32[48,2048]{1,0:T(8,128)S(1)}, f32[48,2048]{1,0:T(8,128)S(1)}, u32[]{:S(2)}, u32[]{:S(2)}) collective-permute-start(f32[48,2048]{1,0:T(8,128)S(1)} %get-tuple-element.69), channel_id=1, source_target_pairs={{0,2},{1,135},{2,4},{3,1},{4,6},{5,3},{6,128},{7,5},{128,130},{129... | collective-permute-start | bytes 1179656 | tf_op jit(solution)/shard_map/ppermute | solution.py:43
  21.7 3.4 %copy-start = (f32[256,8192]{1,0:T(8,128)S(1)}, f32[256,8192]{1,0:T(8,128)}, u32[]{:S(2)}) copy-start(f32[256,8192]{1,0:T(8,128)} %refs_0_.1) | copy-start | bytes 25165828
  25.5 8.4 %collective-permute-start.16 = (f32[64,2048]{1,0:T(8,128)S(1)}, f32[64,2048]{1,0:T(8,128)S(1)}, u32[]{:S(2)}, u32[]{:S(2)}) collective-permute-start(f32[64,2048]{1,0:T(8,128)S(1)} %get-tuple-element.84), channel_id=1, source_target_pairs={{0,8},{1,25},{2,10},{3,27},{4,12},{5,29},{6,14},{7,31},{128,136},{... | collective-permute-start | bytes 1572872 | tf_op jit(solution)/shard_map/ppermute | solution.py:43
  25.8 8.3 %collective-permute-start.17 = (f32[64,2048]{1,0:T(8,128)S(1)}, f32[64,2048]{1,0:T(8,128)S(1)}, u32[]{:S(2)}, u32[]{:S(2)}) collective-permute-start(f32[64,2048]{1,0:T(8,128)S(1)} %get-tuple-element.85), channel_id=1, source_target_pairs={{0,2},{1,135},{2,4},{3,1},{4,6},{5,3},{6,128},{7,5},{128,130},{129... | collective-permute-start | bytes 1572872 | tf_op jit(solution)/shard_map/ppermute | solution.py:43
  27.8 16.5 %slice-start = ((s8[8388608]{0:T(1024)(128)(4,1)}), s8[4194304]{0:T(1024)(128)(4,1)S(1)}, s32[]{:S(2)}) async-start(s8[8388608]{0:T(1024)(128)(4,1)} %bitcast.3), calls=%async_computation | async-start | bytes 8388608
  27.9 11.6 %collective-permute-start.4 = (f32[64,2048]{1,0:T(8,128)S(1)}, f32[64,2048]{1,0:T(8,128)S(1)}, u32[]{:S(2)}, u32[]{:S(2)}) collective-permute-start(f32[64,2048]{1,0:T(8,128)S(1)} %get-tuple-element.70), channel_id=1, source_target_pairs={{0,8},{1,25},{2,10},{3,27},{4,12},{5,29},{6,14},{7,31},{128,136},{... | collective-permute-start | bytes 1572872 | tf_op jit(solution)/shard_map/ppermute | solution.py:43
  28.3 11.4 %collective-permute-start.5 = (f32[64,2048]{1,0:T(8,128)S(1)}, f32[64,2048]{1,0:T(8,128)S(1)}, u32[]{:S(2)}, u32[]{:S(2)}) collective-permute-start(f32[64,2048]{1,0:T(8,128)S(1)} %get-tuple-element.71), channel_id=1, source_target_pairs={{0,2},{1,135},{2,4},{3,1},{4,6},{5,3},{6,128},{7,5},{128,130},{129... | collective-permute-start | bytes 1572872 | tf_op jit(solution)/shard_map/ppermute | solution.py:43
  34.2 8.6 %copy-start.4 = (s32[256]{0:T(256)S(1)}, s32[256]{0:T(256)}, u32[]{:S(2)}) copy-start(s32[256]{0:T(256)} %param.11) | copy-start | bytes 3076
  34.2 8.6 %copy-start.5 = (f32[256]{0:T(256)S(1)}, f32[256]{0:T(256)}, u32[]{:S(2)}) copy-start(f32[256]{0:T(256)} %param.10) | copy-start | bytes 3076
  34.2 10.1 %slice-start.1 = ((s8[8388608]{0:T(1024)(128)(4,1)}), s8[4194304]{0:T(1024)(128)(4,1)S(1)}, s32[]{:S(2)}) async-start(s8[8388608]{0:T(1024)(128)(4,1)} %bitcast.3), calls=%async_computation.1 | async-start | bytes 8388608
  34.2 10.4 %collective-permute-start.20 = (f32[48,2048]{1,0:T(8,128)S(1)}, f32[48,2048]{1,0:T(8,128)S(1)}, u32[]{:S(2)}, u32[]{:S(2)}) collective-permute-start(f32[48,2048]{1,0:T(8,128)S(1)} %get-tuple-element.89), channel_id=1, source_target_pairs={{0,2},{1,135},{2,4},{3,1},{4,6},{5,3},{6,128},{7,5},{128,130},{129... | collective-permute-start | bytes 1179656 | tf_op jit(solution)/shard_map/ppermute | solution.py:43
  37.4 7.3 %collective-permute-start.19 = (f32[48,2048]{1,0:T(8,128)S(1)}, f32[48,2048]{1,0:T(8,128)S(1)}, u32[]{:S(2)}, u32[]{:S(2)}) collective-permute-start(f32[48,2048]{1,0:T(8,128)S(1)} %get-tuple-element.88), channel_id=1, source_target_pairs={{0,8},{1,25},{2,10},{3,27},{4,12},{5,29},{6,14},{7,31},{128,136},{... | collective-permute-start | bytes 1179656 | tf_op jit(solution)/shard_map/ppermute | solution.py:43
  39.8 8.8 %collective-permute-start.6 = (f32[48,2048]{1,0:T(8,128)S(1)}, f32[48,2048]{1,0:T(8,128)S(1)}, u32[]{:S(2)}, u32[]{:S(2)}) collective-permute-start(f32[48,2048]{1,0:T(8,128)S(1)} %get-tuple-element.72), channel_id=1, source_target_pairs={{0,8},{1,25},{2,10},{3,27},{4,12},{5,29},{6,14},{7,31},{128,136},{... | collective-permute-start | bytes 1179656 | tf_op jit(solution)/shard_map/ppermute | solution.py:43
  41.3 7.3 %collective-permute-start.7 = (f32[48,2048]{1,0:T(8,128)S(1)}, f32[48,2048]{1,0:T(8,128)S(1)}, u32[]{:S(2)}, u32[]{:S(2)}) collective-permute-start(f32[48,2048]{1,0:T(8,128)S(1)} %get-tuple-element.73), channel_id=1, source_target_pairs={{0,2},{1,135},{2,4},{3,1},{4,6},{5,3},{6,128},{7,5},{128,130},{129... | collective-permute-start | bytes 1179656 | tf_op jit(solution)/shard_map/ppermute | solution.py:43
  44.8 9.0 %collective-permute-start.21 = (f32[32,2048]{1,0:T(8,128)S(1)}, f32[32,2048]{1,0:T(8,128)S(1)}, u32[]{:S(2)}, u32[]{:S(2)}) collective-permute-start(f32[32,2048]{1,0:T(8,128)S(1)} %get-tuple-element.96), channel_id=1, source_target_pairs={{0,8},{1,25},{2,10},{3,27},{4,12},{5,29},{6,14},{7,31},{128,136},{... | collective-permute-start | bytes 786440 | tf_op jit(solution)/shard_map/ppermute | solution.py:43
  47.5 6.3 %collective-permute-start.22 = (f32[32,2048]{1,0:T(8,128)S(1)}, f32[32,2048]{1,0:T(8,128)S(1)}, u32[]{:S(2)}, u32[]{:S(2)}) collective-permute-start(f32[32,2048]{1,0:T(8,128)S(1)} %get-tuple-element.97), channel_id=1, source_target_pairs={{0,2},{1,135},{2,4},{3,1},{4,6},{5,3},{6,128},{7,5},{128,130},{129... | collective-permute-start | bytes 786440 | tf_op jit(solution)/shard_map/ppermute | solution.py:43
  48.7 7.6 %collective-permute-start.8 = (f32[32,2048]{1,0:T(8,128)S(1)}, f32[32,2048]{1,0:T(8,128)S(1)}, u32[]{:S(2)}, u32[]{:S(2)}) collective-permute-start(f32[32,2048]{1,0:T(8,128)S(1)} %get-tuple-element.74), channel_id=1, source_target_pairs={{0,8},{1,25},{2,10},{3,27},{4,12},{5,29},{6,14},{7,31},{128,136},{... | collective-permute-start | bytes 786440 | tf_op jit(solution)/shard_map/ppermute | solution.py:43
  50.3 6.4 %collective-permute-start.9 = (f32[32,2048]{1,0:T(8,128)S(1)}, f32[32,2048]{1,0:T(8,128)S(1)}, u32[]{:S(2)}, u32[]{:S(2)}) collective-permute-start(f32[32,2048]{1,0:T(8,128)S(1)} %get-tuple-element.75), channel_id=1, source_target_pairs={{0,2},{1,135},{2,4},{3,1},{4,6},{5,3},{6,128},{7,5},{128,130},{129... | collective-permute-start | bytes 786440 | tf_op jit(solution)/shard_map/ppermute | solution.py:43
  53.9 6.6 %collective-permute-start.23 = (f32[16,2048]{1,0:T(8,128)S(1)}, f32[16,2048]{1,0:T(8,128)S(1)}, u32[]{:S(2)}, u32[]{:S(2)}) collective-permute-start(f32[16,2048]{1,0:T(8,128)S(1)} %get-tuple-element.101), channel_id=1, source_target_pairs={{0,8},{1,25},{2,10},{3,27},{4,12},{5,29},{6,14},{7,31},{128,136},{... | collective-permute-start | bytes 393224 | tf_op jit(solution)/shard_map/ppermute | solution.py:43
  54.4 6.1 %collective-permute-start.24 = (f32[16,2048]{1,0:T(8,128)S(1)}, f32[16,2048]{1,0:T(8,128)S(1)}, u32[]{:S(2)}, u32[]{:S(2)}) collective-permute-start(f32[16,2048]{1,0:T(8,128)S(1)} %get-tuple-element.102), channel_id=1, source_target_pairs={{0,2},{1,135},{2,4},{3,1},{4,6},{5,3},{6,128},{7,5},{128,130},{129... | collective-permute-start | bytes 393224 | tf_op jit(solution)/shard_map/ppermute | solution.py:43
  56.8 8.9 %collective-permute-start.10 = (f32[16,2048]{1,0:T(8,128)S(1)}, f32[16,2048]{1,0:T(8,128)S(1)}, u32[]{:S(2)}, u32[]{:S(2)}) collective-permute-start(f32[16,2048]{1,0:T(8,128)S(1)} %get-tuple-element.76), channel_id=1, source_target_pairs={{0,8},{1,25},{2,10},{3,27},{4,12},{5,29},{6,14},{7,31},{128,136},{... | collective-permute-start | bytes 393224 | tf_op jit(solution)/shard_map/ppermute | solution.py:43
  57.3 8.3 %collective-permute-start.11 = (f32[16,2048]{1,0:T(8,128)S(1)}, f32[16,2048]{1,0:T(8,128)S(1)}, u32[]{:S(2)}, u32[]{:S(2)}) collective-permute-start(f32[16,2048]{1,0:T(8,128)S(1)} %get-tuple-element.77), channel_id=1, source_target_pairs={{0,2},{1,135},{2,4},{3,1},{4,6},{5,3},{6,128},{7,5},{128,130},{129... | collective-permute-start | bytes 393224 | tf_op jit(solution)/shard_map/ppermute | solution.py:43
  65.6 57.3 %copy-start.3 = (f32[8,2,8192]{2,1,0:T(2,128)S(1)}, f32[8,2,8192]{2,1,0:T(2,128)}, u32[]{:S(2)}) copy-start(f32[8,2,8192]{2,1,0:T(2,128)} %refs_4_.1) | copy-start | bytes 1572868
  70.2 53.9 %copy-start.2 = (f32[8,2,8192]{2,1,0:T(2,128)S(1)}, f32[8,2,8192]{2,1,0:T(2,128)}, u32[]{:S(2)}) copy-start(f32[8,2,8192]{2,1,0:T(2,128)} %refs_5_.1) | copy-start | bytes 1572868
  70.2 53.8 %copy-start.6 = (f32[64]{0:T(128)S(1)}, f32[64]{0:T(128)}, u32[]{:S(2)}) copy-start(f32[64]{0:T(128)} %param.9) | copy-start | bytes 772
  70.3 6.4 %collective-permute-start.25 = (f32[2,2,2,2,8,256]{5,4,3,2,1,0:T(8,128)S(1)}, f32[2,2,2,2,8,256]{5,4,3,2,1,0:T(8,128)S(1)}, u32[]{:S(2)}, u32[]{:S(2)}) collective-permute-start(f32[2,2,2,2,8,256]{5,4,3,2,1,0:T(8,128)S(1)} %get-tuple-element.106), channel_id=1, source_target_pairs={{0,32},{1,33},{2,34},{3,35},{4,36},{5,37},{6,38},{7,39},{128,160},... | collective-permute-start | bytes 393224 | tf_op jit(solution)/shard_map/ppermute | solution.py:43
  71.5 7.3 %collective-permute-start.26 = (f32[2,2,2,2,8,256]{5,4,3,2,1,0:T(8,128)S(1)}, f32[2,2,2,2,8,256]{5,4,3,2,1,0:T(8,128)S(1)}, u32[]{:S(2)}, u32[]{:S(2)}) collective-permute-start(f32[2,2,2,2,8,256]{5,4,3,2,1,0:T(8,128)S(1)} %get-tuple-element.107), channel_id=1, source_target_pairs={{0,64},{1,65},{2,66},{3,67},{4,68},{5,69},{6,70},{7,71},{128,192},... | collective-permute-start | bytes 393224 | tf_op jit(solution)/shard_map/ppermute | solution.py:43
  74.0 4.9 %collective-permute-start.27 = (f32[2,2,2,2,8,256]{5,4,3,2,1,0:T(8,128)S(1)}, f32[2,2,2,2,8,256]{5,4,3,2,1,0:T(8,128)S(1)}, u32[]{:S(2)}, u32[]{:S(2)}) collective-permute-start(f32[2,2,2,2,8,256]{5,4,3,2,1,0:T(8,128)S(1)} %get-tuple-element.108), channel_id=1, source_target_pairs={{0,96},{1,97},{2,98},{3,99},{4,100},{5,101},{6,102},{7,103},{128,2... | collective-permute-start | bytes 393224 | tf_op jit(solution)/shard_map/ppermute | solution.py:43
  75.1 5.3 %collective-permute-start.28 = (f32[4,2,16,256]{3,2,1,0:T(8,128)S(1)}, f32[4,2,16,256]{3,2,1,0:T(8,128)S(1)}, u32[]{:S(2)}, u32[]{:S(2)}) collective-permute-start(f32[4,2,16,256]{3,2,1,0:T(8,128)S(1)} %get-tuple-element.110), channel_id=1, source_target_pairs={{0,24},{1,9},{2,26},{3,11},{4,28},{5,13},{6,30},{7,15},{128,152},{... | collective-permute-start | bytes 393224 | tf_op jit(solution)/shard_map/ppermute | solution.py:43
  76.4 5.6 %collective-permute-start.29 = (f32[4,2,16,256]{3,2,1,0:T(8,128)S(1)}, f32[4,2,16,256]{3,2,1,0:T(8,128)S(1)}, u32[]{:S(2)}, u32[]{:S(2)}) collective-permute-start(f32[4,2,16,256]{3,2,1,0:T(8,128)S(1)} %get-tuple-element.111), channel_id=1, source_target_pairs={{0,16},{1,17},{2,18},{3,19},{4,20},{5,21},{6,22},{7,23},{128,144},... | collective-permute-start | bytes 393224 | tf_op jit(solution)/shard_map/ppermute | solution.py:43
  76.6 5.8 %collective-permute-start.30 = (f32[4,2,16,256]{3,2,1,0:T(8,128)S(1)}, f32[4,2,16,256]{3,2,1,0:T(8,128)S(1)}, u32[]{:S(2)}, u32[]{:S(2)}) collective-permute-start(f32[4,2,16,256]{3,2,1,0:T(8,128)S(1)} %get-tuple-element.112), channel_id=1, source_target_pairs={{0,8},{1,25},{2,10},{3,27},{4,12},{5,29},{6,14},{7,31},{128,136},{... | collective-permute-start | bytes 393224 | tf_op jit(solution)/shard_map/ppermute | solution.py:43
  82.7 17.7 %collective-permute-start.35 = (f32[12,2,8,256]{3,2,1,0:T(8,128)S(1)}, f32[12,2,8,256]{3,2,1,0:T(8,128)S(1)}, u32[]{:S(2)}, u32[]{:S(2)}) collective-permute-start(f32[12,2,8,256]{3,2,1,0:T(8,128)S(1)} %get-tuple-element.118), channel_id=1, source_target_pairs={{0,130},{1,7},{2,132},{3,129},{4,134},{5,131},{6,0},{7,133},{128,2... | collective-permute-start | bytes 589832 | tf_op jit(solution)/shard_map/ppermute | solution.py:43
  82.8 17.6 %collective-permute-start.36 = (f32[12,2,8,256]{3,2,1,0:T(8,128)S(1)}, f32[12,2,8,256]{3,2,1,0:T(8,128)S(1)}, u32[]{:S(2)}, u32[]{:S(2)}) collective-permute-start(f32[12,2,8,256]{3,2,1,0:T(8,128)S(1)} %get-tuple-element.119), channel_id=1, source_target_pairs={{0,132},{1,5},{2,134},{3,7},{4,0},{5,129},{6,2},{7,131},{128,4},{1... | collective-permute-start | bytes 589832 | tf_op jit(solution)/shard_map/ppermute | solution.py:43
  82.9 17.4 %collective-permute-start.37 = (f32[12,2,8,256]{3,2,1,0:T(8,128)S(1)}, f32[12,2,8,256]{3,2,1,0:T(8,128)S(1)}, u32[]{:S(2)}, u32[]{:S(2)}) collective-permute-start(f32[12,2,8,256]{3,2,1,0:T(8,128)S(1)} %get-tuple-element.120), channel_id=1, source_target_pairs={{0,134},{1,3},{2,0},{3,5},{4,2},{5,7},{6,4},{7,129},{128,6},{129,1... | collective-permute-start | bytes 589832 | tf_op jit(solution)/shard_map/ppermute | solution.py:43
  84.8 4.3 %collective-permute-start.31 = (f32[4,2,8,256]{3,2,1,0:T(8,128)S(1)}, f32[4,2,8,256]{3,2,1,0:T(8,128)S(1)}, u32[]{:S(2)}, u32[]{:S(2)}) collective-permute-start(f32[4,2,8,256]{3,2,1,0:T(8,128)S(1)} %get-tuple-element.114), channel_id=1, source_target_pairs={{0,2},{1,135},{2,4},{3,1},{4,6},{5,3},{6,128},{7,5},{128,130},{129... | collective-permute-start | bytes 196616 | tf_op jit(solution)/shard_map/ppermute | solution.py:43
  86.7 5.5 %collective-permute-start.32 = (f32[4,2,8,256]{3,2,1,0:T(8,128)S(1)}, f32[4,2,8,256]{3,2,1,0:T(8,128)S(1)}, u32[]{:S(2)}, u32[]{:S(2)}) collective-permute-start(f32[4,2,8,256]{3,2,1,0:T(8,128)S(1)} %get-tuple-element.115), channel_id=1, source_target_pairs={{0,4},{1,133},{2,6},{3,135},{4,128},{5,1},{6,130},{7,3},{128,132},... | collective-permute-start | bytes 196616 | tf_op jit(solution)/shard_map/ppermute | solution.py:43
  89.1 6.2 %collective-permute-start.33 = (f32[4,2,8,256]{3,2,1,0:T(8,128)S(1)}, f32[4,2,8,256]{3,2,1,0:T(8,128)S(1)}, u32[]{:S(2)}, u32[]{:S(2)}) collective-permute-start(f32[4,2,8,256]{3,2,1,0:T(8,128)S(1)} %get-tuple-element.116), channel_id=1, source_target_pairs={{0,6},{1,131},{2,128},{3,133},{4,130},{5,135},{6,132},{7,1},{128,1... | collective-permute-start | bytes 196616 | tf_op jit(solution)/shard_map/ppermute | solution.py:43
  92.3 8.1 %collective-permute-start.34 = (f32[4,2,8,256]{3,2,1,0:T(8,128)S(1)}, f32[4,2,8,256]{3,2,1,0:T(8,128)S(1)}, u32[]{:S(2)}, u32[]{:S(2)}) collective-permute-start(f32[4,2,8,256]{3,2,1,0:T(8,128)S(1)} %get-tuple-element.117), channel_id=1, source_target_pairs={{0,128},{1,129},{2,130},{3,131},{4,132},{5,133},{6,134},{7,135},{1... | collective-permute-start | bytes 196616 | tf_op jit(solution)/shard_map/ppermute | solution.py:43
  100.7 5.4 %collective-permute-start.38 = (f32[4,2,2,8,256]{4,3,2,1,0:T(8,128)S(1)}, f32[4,2,2,8,256]{4,3,2,1,0:T(8,128)S(1)}, u32[]{:S(2)}, u32[]{:S(2)}) collective-permute-start(f32[4,2,2,8,256]{4,3,2,1,0:T(8,128)S(1)} %get-tuple-element.122), channel_id=1, source_target_pairs={{0,8},{1,9},{2,10},{3,11},{4,12},{5,13},{6,14},{7,15},{128,136},{1... | collective-permute-start | bytes 393224 | tf_op jit(solution)/shard_map/ppermute | solution.py:43
  100.8 7.7 %collective-permute-start.39 = (f32[4,2,2,8,256]{4,3,2,1,0:T(8,128)S(1)}, f32[4,2,2,8,256]{4,3,2,1,0:T(8,128)S(1)}, u32[]{:S(2)}, u32[]{:S(2)}) collective-permute-start(f32[4,2,2,8,256]{4,3,2,1,0:T(8,128)S(1)} %get-tuple-element.123), channel_id=1, source_target_pairs={{0,16},{1,17},{2,18},{3,19},{4,20},{5,21},{6,22},{7,23},{128,144},... | collective-permute-start | bytes 393224 | tf_op jit(solution)/shard_map/ppermute | solution.py:43
  104.7 4.1 %collective-permute-start.40 = (f32[4,2,2,8,256]{4,3,2,1,0:T(8,128)S(1)}, f32[4,2,2,8,256]{4,3,2,1,0:T(8,128)S(1)}, u32[]{:S(2)}, u32[]{:S(2)}) collective-permute-start(f32[4,2,2,8,256]{4,3,2,1,0:T(8,128)S(1)} %get-tuple-element.124), channel_id=1, source_target_pairs={{0,24},{1,25},{2,26},{3,27},{4,28},{5,29},{6,30},{7,31},{128,152},... | collective-permute-start | bytes 393224 | tf_op jit(solution)/shard_map/ppermute | solution.py:43
  108.9 15.2 %collective-permute-start.41 = (f32[4,4,2,8,256]{4,3,2,1,0:T(8,128)S(1)}, f32[4,4,2,8,256]{4,3,2,1,0:T(8,128)S(1)}, u32[]{:S(2)}, u32[]{:S(2)}) collective-permute-start(f32[4,4,2,8,256]{4,3,2,1,0:T(8,128)S(1)} %swap_pack.1), channel_id=1, source_target_pairs={{0,1},{1,0},{2,3},{3,2},{4,5},{5,4},{6,7},{7,6},{128,129},{129,128... | collective-permute-start | bytes 786440 | tf_op jit(solution)/shard_map/ppermute | solution.py:43
